TPU v7x, 32 devices: a whole 2x2x4 slice. The times are simulated.
32 devices in a mesh: groups: 2 (over y), samples: 4 (over z), blocks: 2 (over x), folds: 2 (over core).
Axes of the slice: x: 2, y: 2, z: 4, core: 2. Of those that a mesh axis runs over, the one named last changes fastest.
Arguments:
- allele_dosage_table: bfloat16 [1000, 4096], P('blocks', ('groups', 'samples')), parts along dimension 1, may hold values from -6 to 6
- phenotype_values: bfloat16 [20, 4096], P(None, ('groups', 'samples')), parts along dimension 1, may hold values from -8 to 8
- individual_partition_label: int32 [4096], P(('groups', 'samples')), parts along dimension 0, may hold values from 0 to 3, as said below
- shrink_strengths: float32 [2], replicated, may hold values from 0.005 to 2, as said below
Outputs:
- predictions: bfloat16 [4, 2, 2, 20, 1024], P('folds', 'blocks', None, None, ('groups', 'samples')), parts along dimension 4
- level_gram: float32 [8, 2, 2, 20, 2, 2], P(('groups', 'folds'), 'blocks'), parts along dimension 0
- level_cross: float32 [8, 2, 2, 20], P(('groups', 'folds'), 'blocks'), parts along dimension 0
There are 2 independent parts, one for each index of `groups`. A program takes and returns all parts, laid end to end along the dimension named above; an argument that names none is the same for every part. Nothing has to cross between parts.
Inputs may be any that keep to these rules, and one draw needn't show every extreme that they name: `individual_partition_label`: among the 512 samples of each device (aligned runs of 512 indices) every fold number appears equally often, 512 / 4 times. `shrink_strengths`: the first penalty lies between 0.005 and 0.02, every other one between 0.1 and 2.
All inputs are finite; a program needn't handle non-finite values.
Results may differ from a plain program's by a relative error of at most 0.0055.
Values may be sent and summed in bfloat16 or wider, within the bound.
A program may use at most 64 MiB of HBM per device.

v0:
```python
import jax
import jax.numpy as jnp
from jax import lax
from jax.sharding import PartitionSpec as P

SHRINK_LEVELS = 2
FOLDS = 4


def per_device(allele_dosage_table, phenotype_values, individual_partition_label, shrink_strengths):
    own_count = FOLDS // lax.axis_size("folds")
    first = lax.axis_index("folds") * own_count
    rows_fold = allele_dosage_table.shape[1] // FOLDS
    total_rows = lax.axis_size("samples") * allele_dosage_table.shape[1]
    held_rows = total_rows // FOLDS
    learning_individual_tally = total_rows - held_rows
    sample_order = jnp.argsort(individual_partition_label, stable=True).reshape(FOLDS, rows_fold)
    geno_sorted = jnp.take(allele_dosage_table, sample_order, axis=1)
    trait_sorted = jnp.take(phenotype_values, sample_order, axis=1)
    geno_own = lax.dynamic_slice_in_dim(geno_sorted, first, own_count, 1)
    trait_own = lax.dynamic_slice_in_dim(trait_sorted, first, own_count, 1)
    held_gram = jnp.einsum(
        "bki,cki->kbc", geno_sorted, geno_sorted, preferred_element_type=jnp.float32
    )
    held_cross = jnp.einsum(
        "bki,pki->kbp", geno_sorted, trait_sorted, preferred_element_type=jnp.float32
    )
    own_gram = lax.dynamic_slice_in_dim(held_gram, first, own_count, 0)
    own_cross = lax.dynamic_slice_in_dim(held_cross, first, own_count, 0)
    learning_design_inner, learning_design_response = lax.psum(
        (jnp.sum(held_gram, 0)[None] - own_gram, jnp.sum(held_cross, 0)[None] - own_cross),
        "samples",
    )
    pair_total = own_count * SHRINK_LEVELS
    sample_devices = lax.axis_size("samples")
    per_processor = (pair_total + sample_devices - 1) // sample_devices
    pair_start = lax.axis_index("samples") * per_processor
    pair_ids = jnp.minimum(pair_start + jnp.arange(per_processor, dtype=jnp.int32), pair_total - 1)
    identity = jnp.eye(learning_design_inner.shape[-1], dtype=jnp.float32)

    def one_pair(pair):
        fold_pick = pair // SHRINK_LEVELS
        ridge_pick = pair % SHRINK_LEVELS
        gram_one = lax.dynamic_index_in_dim(learning_design_inner, fold_pick, 0, keepdims=False)
        cross_one = lax.dynamic_index_in_dim(learning_design_response, fold_pick, 0, keepdims=False)
        value = lax.dynamic_index_in_dim(shrink_strengths, ridge_pick, 0, keepdims=False)
        factor = jnp.linalg.cholesky(gram_one / learning_individual_tally + value * identity)
        inner = lax.linalg.triangular_solve(
            factor, cross_one / learning_individual_tally, left_side=True, lower=True
        )
        return lax.linalg.triangular_solve(
            factor, inner, left_side=True, lower=True, transpose_a=True
        )

    local_betas = lax.map(one_pair, pair_ids).astype(jnp.bfloat16)
    gathered = lax.all_gather(local_betas, "samples", axis=0, tiled=True)[:pair_total]
    shaped = gathered.reshape(own_count, SHRINK_LEVELS, gathered.shape[1], gathered.shape[2])
    coefficient_half = jnp.transpose(shaped, (1, 0, 2, 3))
    preds = jnp.einsum(
        "rkbp,bki->krpi", coefficient_half, geno_own, preferred_element_type=jnp.float32
    ).astype(jnp.bfloat16)
    block_preds = preds[:, None]
    contrib = jnp.einsum(
        "krpi,kbspi->krpbs",
        preds,
        lax.all_gather(block_preds, "blocks", axis=1, tiled=True),
        preferred_element_type=jnp.float32,
    )
    cross_rows = jnp.einsum("krpi,pki->krp", preds, trait_own, preferred_element_type=jnp.float32)
    gram_sum, cross_sum = lax.psum((contrib, cross_rows), "samples")
    level_gram = gram_sum[:, None] / held_rows
    level_cross = cross_sum[:, None] / held_rows
    return (block_preds, level_gram, level_cross)


def solution(mesh):
    in_specs = (
        P("blocks", ("groups", "samples")),
        P(None, ("groups", "samples")),
        P(("groups", "samples")),
        P(),
    )
    out_specs = (
        P("folds", "blocks", None, None, ("groups", "samples")),
        P(("groups", "folds"), "blocks", None, None, None, None),
        P(("groups", "folds"), "blocks", None, None),
    )
    return jax.shard_map(
        per_device, mesh=mesh, in_specs=in_specs, out_specs=out_specs, check_vma=False
    )
```

profile of v0, /device:TPU:0, one launch (start us, length us, event | category | flops | bytes accessed | tf_op | source)
XLA Modules:
  0.0 297.7 jit_solution(9942449200774352123)
XLA Ops:
  7.2 4.4 %sort.17 = (s32[512]{0:T(512)}, s32[512]{0:T(512)S(1)}) sort(s32[512]{0:T(512)} %param.6, s32[512]{0:T(512)S(1)} %iota.110), dimensions={0}, to_apply=%region_0.0 | sort | flops 4608 | bytes 8192 | tf_op jit(solution)/shard_map/jit(argsort)/sort | solution.py:17
  11.7 1.2 copy.26
  12.9 2.0 gather_fusion
  14.9 0.3 copy.27
  15.3 2.7 fusion.63
  18.2 1.5 gather_fusion.1
  19.8 0.4 fusion.64
  20.2 3.3 %dynamic-slice_subtract_fusion = f32[2,500,500]{2,1,0:T(8,128)} fusion(f32[4,500,500]{2,1,0:T(8,128)} %get-tuple-element.68, s32[]{:T(128)S(6)} %select_n.66, f32[500,500]{1,0:T(8,128)S(1)} %get-tuple-element.67), kind=kLoop, calls=%fused_computation.4 | loop fusion | flops 500000 | bytes 5000004 | tf_op jit(solution)/shard_map/sub | solution.py:31
  23.5 0.6 dynamic-slice_subtract_fusion.1
  24.2 0.6 dynamic_slice.32
  24.8 91.6 %all-reduce.7.cloned.1.call-done = (f32[2,500,500]{2,1,0:T(8,128)}, f32[2,500,20]{1,2,0:T(8,128)}) async-done(((f32[2,500,500]{2,1,0:T(8,128)}, f32[2,500,20]{1,2,0:T(8,128)}), (f32[2,500,500]{2,1,0:T(8,128)}, f32[2,500,20]{1,2,0:T(8,128)})) %all-reduce.7.cloned.1.call-update) | async-done | bytes 2080016 | tf_op jit(solution)/shard_map/psum | solution.py:30
  116.5 2.0 bitcast_add_fusion.1
  118.5 0.3 copy.28
  118.8 2.1 fusion.1
  121.0 11.7 %cholesky.104 = f32[128,128]{1,0:T(8,128)S(1)} custom-call(f32[128,128]{1,0:T(8,128)S(1)} %cholesky.269), custom_call_target="Cholesky" | custom-call | tf_op jit(solution)/shard_map/while/body/eval_jaxpr/jit(cholesky)/cholesky | solution.py:47
  132.8 9.8 %custom-call.40 = f32[1,128,128]{1,2,0:T(8,128)S(1)} custom-call(f32[1,128,128]{2,1,0:T(8,128)S(1)} %get-tuple-element.64), custom_call_target="InvertDiagBlocksLowerTriangular" | custom-call | tf_op jit(solution)/shard_map/while/body/eval_jaxpr/jit(cholesky)/cholesky | solution.py:47
  142.7 0.5 constant_dynamic-update-slice_fusion
  143.1 0.5 convolution_subtract_fusion
  143.6 11.7 %cholesky.217 = f32[128,128]{1,0:T(8,128)S(1)} custom-call(f32[128,128]{1,0:T(8,128)S(1)} %cholesky.273), custom_call_target="Cholesky" | custom-call | tf_op jit(solution)/shard_map/while/body/eval_jaxpr/jit(cholesky)/cholesky | solution.py:47
  155.4 9.9 %custom-call.41 = f32[1,128,128]{1,2,0:T(8,128)S(1)} custom-call(f32[1,128,128]{2,1,0:T(8,128)S(1)} %get-tuple-element.61), custom_call_target="InvertDiagBlocksLowerTriangular" | custom-call | tf_op jit(solution)/shard_map/while/body/eval_jaxpr/jit(cholesky)/cholesky | solution.py:47
  165.3 0.4 convolution_dynamic-update-slice_fusion
  165.7 0.4 convolution_subtract_fusion.1
  166.1 11.7 %cholesky.238 = f32[128,128]{1,0:T(8,128)S(1)} custom-call(f32[128,128]{1,0:T(8,128)S(1)} %cholesky.278), custom_call_target="Cholesky" | custom-call | tf_op jit(solution)/shard_map/while/body/eval_jaxpr/jit(cholesky)/cholesky | solution.py:47
  177.8 9.8 %custom-call.42 = f32[1,128,128]{1,2,0:T(8,128)S(1)} custom-call(f32[1,128,128]{2,1,0:T(8,128)S(1)} %get-tuple-element.58), custom_call_target="InvertDiagBlocksLowerTriangular" | custom-call | tf_op jit(solution)/shard_map/while/body/eval_jaxpr/jit(cholesky)/cholesky | solution.py:47
  187.6 0.3 convolution_dynamic-update-slice_fusion.1
  187.9 0.4 convolution_subtract_fusion.2
  188.3 10.8 %cholesky.258 = f32[116,116]{1,0:T(8,128)S(1)} custom-call(f32[116,116]{1,0:T(8,128)S(1)} %convolution_subtract_fusion.2), custom_call_target="Cholesky" | custom-call | tf_op jit(solution)/shard_map/while/body/eval_jaxpr/jit(cholesky)/cholesky | solution.py:47
  199.1 0.7 compare_reduce_fusion.1
  199.9 0.6 compare_reduce_fusion
  200.5 0.6 compare_reduce_fusion.2
  203.8 6.0 %while.1 = (s32[]{:T(128)}, f32[500,500]{1,0:T(8,128)S(1)}, s32[3,2]{0,1:T(2,128)S(1)}, f32[3,128,128]{2,1,0:T(8,128)S(1)}, s32[]{:T(128)}) while((s32[]{:T(128)}, f32[500,500]{1,0:T(8,128)S(1)}, s32[3,2]{0,1:T(2,128)S(1)}, f32[3,128,128]{2,1,0:T(8,128)S(1)}, s32[]{:T(128)}) %tuple.38), condition=%wide.while_cond, body=%wide.while_body.sunk | while | flops 2 | bytes 131189 | solution.py:51
  203.9 0.5 fusion.77
  204.4 1.4 bitcast_dynamic-update-slice_fusion.2
  205.9 0.5 fusion.77
  206.4 1.4 bitcast_dynamic-update-slice_fusion.2
  207.9 0.5 fusion.77
  208.4 1.4 bitcast_dynamic-update-slice_fusion.2
  210.0 39.3 %custom-call.43 = f32[4,128,128]{1,2,0:T(8,128)S(1)} custom-call(f32[4,128,128]{2,1,0:T(8,128)S(1)} %pad_maximum_fusion), custom_call_target="InvertDiagBlocksLowerTriangular" | custom-call | tf_op jit(solution)/shard_map/while/body/eval_jaxpr/triangular_solve | solution.py:51
  250.3 0.3 convolution_subtract_fusion.6
  250.6 0.2 fusion.32
  251.7 0.2 fusion.25
  251.9 0.2 convolution_subtract_fusion.3
  252.4 13.4 %all_gather.6 = bf16[4,500,20]{1,2,0:T(8,128)(2,1)S(1)} all-gather(bf16[1,500,20]{1,2,0:T(8,128)(2,1)S(1)} %pad_maximum_fusion.1), channel_id=1, replica_groups=mesh['groups'=2,'samples'=4,'blocks'=2,'folds'=2] {'samples'}, dimensions={0}, use_global_device_ids=true | all-gather | bytes 100000 | tf_op jit(solution)/shard_map/all_gather | solution.py:56
  266.0 4.5 %all-gather = bf16[2,4,20,128]{3,2,1,0:T(8,128)(2,1)S(1)} all-gather(bf16[2,2,20,128]{3,2,1,0:T(8,128)(2,1)S(1)} %convolution_convert_fusion), channel_id=2, replica_groups=mesh['groups'=2,'samples'=4,'blocks'=2,'folds'=2] {'blocks'}, dimensions={1}, use_global_device_ids=true | all-gather | bytes 61440 | tf_op jit(solution)/shard_map/all_gather | solution.py:66
  270.5 0.6 copy.33
  271.6 17.9 %all-reduce.3 = (f32[2,2,20,2,2]{1,4,3,2,0:T(2,128)S(1)}, f32[2,2,20]{2,1,0:T(2,128)S(1)}) all-reduce(f32[2,2,20,2,2]{1,4,3,2,0:T(2,128)S(1)} %convolution_bitcast_fusion, f32[2,2,20]{2,1,0:T(2,128)S(1)} %bitcast.149), channel_id=1, replica_groups=mesh['groups'=2,'samples'=4,'blocks'=2,'folds'=2] {'samples'}, use_global_device_ids=true, to_apply=%region_13.14 | all-reduce | flops 400 | bytes 3200 | tf_op jit(solution)/shard_map/psum | solution.py:70
  289.5 0.7 copy.34
  290.2 0.6 multiply_bitcast_fusion.1
  (57 shorter events, 3.9 us)
Async XLA Ops:
  7.2 109.3 %all-reduce.7.cloned.1.call-start = ((), (), s32[]{:S(2)}) async-start(), calls=%async_computation | async-start | bytes 4325376 | tf_op jit(solution)/shard_map/psum | solution.py:30
  15.3 2.8 copy-start
  23.5 0.7 copy-start.2
  187.9 61.4 %copy-start.1 = (f32[2,500,20]{1,2,0:T(8,128)S(1)}, f32[2,500,20]{1,2,0:T(8,128)}, u32[]{:S(2)}) copy-start(f32[2,500,20]{1,2,0:T(8,128)} %get-tuple-element.54) | copy-start | bytes 240004
Sparse Core Ops, SparseCore 0:
  24.3 92.1 all-reduce.6
where the time goes:
time: 298 us
  other arithmetic  131 us (44%)
  waiting for transfers between devices  91.6 us (31%)
  blocking collectives  35.8 us (12%)
  between operations  17.1 us (6%)
  local copies, waits for them, and re-layouts  13.7 us (5%)
  matrix products  8.82 us (3%)
    psum x1, waiting for transfers between devices, per_device(): lax.psum((jnp.sum(held_gram, 0)[None] - own_gram, jnp.sum(held_cross, 0)[...  91.6 us
    another operation x14, other arithmetic, one_pair(): jnp.linalg.cholesky(gram_one / learning_individual_tally + value * identity)  77.6 us
    another operation x11, other arithmetic, one_pair(): lax.linalg.triangular_solve(factor, inner, left_side=True, lower=True, tr...  39.7 us
    psum x1, blocking collectives, per_device(): gram_sum, cross_sum = lax.psum((contrib, cross_rows), 'samples')  17.9 us
    all_gather x1, blocking collectives, per_device(): lax.all_gather(local_betas, 'samples', axis=0, tiled=True)[:pair_total]  13.4 us
  transfers between devices with their start and end apart: 1, of which 1 were waited for; matrix products, arithmetic and copies ran while one was open for 0% of the time, Pallas kernels for 0%

commit v1 on v0

--- a/solution.py
+++ b/solution.py
@@ -1,10 +1,119 @@
+import functools
+
 import jax
 import jax.numpy as jnp
 from jax import lax
+from jax.experimental import pallas as pl
+from jax.experimental.pallas import tpu as pltpu
 from jax.sharding import PartitionSpec as P
 
 SHRINK_LEVELS = 2
 FOLDS = 4
+PANEL = 128
+MINI = 16
+
+
+def dot_f32(a, b):
+    return lax.dot_general(
+        a, b, (((1,), (0,)), ((), ())), precision=lax.Precision.HIGHEST,
+        preferred_element_type=jnp.float32,
+    )
+
+
+def sweep(block, m):
+    low = m * MINI
+    size = block.shape[0]
+    rows = block[low:low + MINI, :]
+    lane = lax.broadcasted_iota(jnp.int32, (MINI, size), 1)
+    sub = lax.broadcasted_iota(jnp.int32, (MINI, size), 0)
+    inside = (lane >= low) & (lane < low + MINI)
+    cols = [jnp.broadcast_to(rows[:, low + j:low + j + 1], (MINI, size)) for j in range(MINI)]
+    run = jnp.where(inside, jnp.where(lane - low == sub, 1.0, 0.0), rows)
+    for j in range(MINI):
+        inv = 1.0 / cols[j][j:j + 1, :]
+        here = sub == j
+        run_j = run[j:j + 1, :] * inv
+        run = jnp.where(here, run_j, run - cols[j] * run_j)
+        for i in range(j + 1, MINI):
+            col_j = cols[i][j:j + 1, :] * inv
+            cols[i] = jnp.where(here, col_j, cols[i] - cols[j] * col_j)
+    lane = lax.broadcasted_iota(jnp.int32, (size, size), 1)
+    sub = lax.broadcasted_iota(jnp.int32, (size, size), 0)
+    in_cols = (lane >= low) & (lane < low + MINI)
+    in_rows = (sub >= low) & (sub < low + MINI)
+    left = jnp.where(in_cols & ~in_rows, block, 0.0)
+    parts = []
+    if low:
+        parts.append(jnp.zeros((low, size), jnp.float32))
+    parts.append(run)
+    if low + MINI < size:
+        parts.append(jnp.zeros((size - low - MINI, size), jnp.float32))
+    placed = jnp.concatenate(parts, axis=0)
+    kept = jnp.where(in_cols | in_rows, 0.0, block)
+    rest = jnp.where(in_rows, placed, kept)
+    return rest - dot_f32(left, placed)
+
+
+def invert(work, strip):
+    size = work.shape[0]
+
+    def panel(p, carry):
+        off = pl.multiple_of(p * PANEL, PANEL)
+        here = pl.ds(off, PANEL)
+        block = work[here, here]
+        for m in range(PANEL // MINI):
+            block = sweep(block, m)
+        sub = lax.broadcasted_iota(jnp.int32, (size, PANEL), 0)
+        col = jnp.where((sub >= off) & (sub < off + PANEL), 0.0, work[:, here])
+        work[:, here] = jnp.zeros((size, PANEL), jnp.float32)
+        strip[...] = dot_f32(block, work[here, :])
+        strip[:, here] = block
+        work[...] = work[...] - dot_f32(col, strip[...])
+        work[here, :] = strip[...]
+        return carry
+
+    lax.fori_loop(0, size // PANEL, panel, 0)
+
+
+def solve_kernel(tally, gram_ref, cross_ref, value_ref, out_ref, matrix, work, strip):
+    size = work.shape[0]
+    count = gram_ref.shape[0]
+    value = value_ref[0]
+    diagonal = lax.broadcasted_iota(jnp.int32, (size, size), 0) == lax.broadcasted_iota(
+        jnp.int32, (size, size), 1
+    )
+    work[...] = jnp.where(diagonal, 1.0, 0.0)
+    gram = gram_ref[...] / tally
+    work[0:count, 0:count] = jnp.where(diagonal[0:count, 0:count], gram + value, gram)
+    matrix[...] = work[...]
+    right = jnp.concatenate(
+        [cross_ref[...] / tally, jnp.zeros((size - count, cross_ref.shape[1]), jnp.float32)], axis=0
+    )
+    invert(work, strip)
+    first = dot_f32(work[...], right)
+    residual = right - dot_f32(matrix[...], first)
+    second = first + dot_f32(work[...], residual)
+    out_ref[...] = second[0:count, :].astype(out_ref.dtype)
+
+
+def ridge_solve(gram, cross, value, tally):
+    size = (gram.shape[0] + PANEL - 1) // PANEL * PANEL
+    return pl.pallas_call(
+        functools.partial(solve_kernel, tally),
+        out_shape=jax.ShapeDtypeStruct(cross.shape, jnp.bfloat16),
+        in_specs=[
+            pl.BlockSpec(memory_space=pltpu.VMEM),
+            pl.BlockSpec(memory_space=pltpu.VMEM),
+            pl.BlockSpec(memory_space=pltpu.SMEM),
+        ],
+        out_specs=pl.BlockSpec(memory_space=pltpu.VMEM),
+        scratch_shapes=[
+            pltpu.VMEM((size, size), jnp.float32),
+            pltpu.VMEM((size, size), jnp.float32),
+            pltpu.VMEM((PANEL, size), jnp.float32),
+        ],
+        compiler_params=pltpu.CompilerParams(vmem_limit_bytes=32 * 1024 * 1024),
+    )(gram, cross, value)
 
 
 def per_device(allele_dosage_table, phenotype_values, individual_partition_label, shrink_strengths):
@@ -36,23 +145,16 @@
     per_processor = (pair_total + sample_devices - 1) // sample_devices
     pair_start = lax.axis_index("samples") * per_processor
     pair_ids = jnp.minimum(pair_start + jnp.arange(per_processor, dtype=jnp.int32), pair_total - 1)
-    identity = jnp.eye(learning_design_inner.shape[-1], dtype=jnp.float32)
 
     def one_pair(pair):
         fold_pick = pair // SHRINK_LEVELS
         ridge_pick = pair % SHRINK_LEVELS
         gram_one = lax.dynamic_index_in_dim(learning_design_inner, fold_pick, 0, keepdims=False)
         cross_one = lax.dynamic_index_in_dim(learning_design_response, fold_pick, 0, keepdims=False)
-        value = lax.dynamic_index_in_dim(shrink_strengths, ridge_pick, 0, keepdims=False)
-        factor = jnp.linalg.cholesky(gram_one / learning_individual_tally + value * identity)
-        inner = lax.linalg.triangular_solve(
-            factor, cross_one / learning_individual_tally, left_side=True, lower=True
-        )
-        return lax.linalg.triangular_solve(
-            factor, inner, left_side=True, lower=True, transpose_a=True
-        )
+        value = lax.dynamic_slice_in_dim(shrink_strengths, ridge_pick, 1)
+        return ridge_solve(gram_one, cross_one, value, float(learning_individual_tally))
 
-    local_betas = lax.map(one_pair, pair_ids).astype(jnp.bfloat16)
+    local_betas = jnp.stack([one_pair(pair_ids[i]) for i in range(per_processor)])
     gathered = lax.all_gather(local_betas, "samples", axis=0, tiled=True)[:pair_total]
     shaped = gathered.reshape(own_count, SHRINK_LEVELS, gathered.shape[1], gathered.shape[2])
     coefficient_half = jnp.transpose(shaped, (1, 0, 2, 3))

time: 298 us -> 189 us (0.63)
  other arithmetic: 131 us -> 9.06 us
  Pallas kernels: 0 us -> 25.1 us
  matrix products: 8.82 us -> 3.68 us
  local copies, waits for them, and re-layouts: 13.7 us -> 8.71 us
    another operation x25 -> x0, other arithmetic: 117 us -> none  [the longest x14 77.6 us: one_pair(): jnp.linalg.cholesky(gram_one / learning_individual_tally + value * identity)]
    pallas_call x0 -> x1, Pallas kernels: none -> 25.1 us  [ridge_solve(): pl.pallas_call(functools.partial(solve_kernel, tally), out_shape=jax.Shap...]
    another operation x15 -> x0, local copies, waits for them, and re-layouts: 6.09 us -> none
    another operation x20 -> x0, matrix products: 5.14 us -> none  [the longest x6 2.28 us: one_pair(): jnp.linalg.cholesky(gram_one / learning_individual_tally + value * identity)]
where the time goes in v1:
time: 189 us; the launch traced here: 188 us
  waiting for transfers between devices  91.7 us (49%)
  blocking collectives  35.8 us (19%)
  Pallas kernels  25.1 us (13%)
  between operations  14.2 us (8%)
  other arithmetic  9.06 us (5%)
  local copies, waits for them, and re-layouts  8.71 us (5%)
  matrix products  3.68 us (2%)
    psum x1, waiting for transfers between devices, per_device(): lax.psum((jnp.sum(held_gram, 0)[None] - own_gram, jnp.sum(held_cross, 0)[...  91.7 us
    pallas_call x1, Pallas kernels, ridge_solve(): pl.pallas_call(functools.partial(solve_kernel, tally), out_shape=jax.Shap...  25.1 us
    psum x1, blocking collectives, per_device(): gram_sum, cross_sum = lax.psum((contrib, cross_rows), 'samples')  17.9 us
    all_gather x1, blocking collectives, per_device(): lax.all_gather(local_betas, 'samples', axis=0, tiled=True)[:pair_total]  13.4 us
    all_gather x1, blocking collectives, per_device(): lax.all_gather(block_preds, 'blocks', axis=1, tiled=True)  4.5 us
    sort x1, other arithmetic, per_device(): jnp.argsort(individual_partition_label, stable=True)  4.45 us
  transfers between devices with their start and end apart: 1, of which 1 were waited for; matrix products, arithmetic and copies ran while one was open for 0% of the time, Pallas kernels for 0%

profile of v1, /device:TPU:0, one launch (start us, length us, event | category | flops | bytes accessed | tf_op | source)
XLA Modules:
  0.0 188.2 jit_solution(15428681830990973773)
XLA Ops:
  7.2 0.0 all-reduce.4.cloned.1.call-start
  7.2 4.4 %sort.17 = (s32[512]{0:T(512)}, s32[512]{0:T(512)S(1)}) sort(s32[512]{0:T(512)} %param.6, s32[512]{0:T(512)S(1)} %iota.4), dimensions={0}, to_apply=%region_0.0 | sort | flops 4608 | bytes 8192 | tf_op jit(solution)/shard_map/jit(argsort)/sort | solution.py:126
  11.7 1.2 copy.28
  12.9 2.0 %gather_fusion = bf16[512,500]{1,0:T(8,128)(2,1)S(1)} fusion(bf16[500,512]{0,1:T(8,128)(2,1)S(1)} %copy.28, s32[1024]{0:T(1024)S(1)} %pad_clamp_fusion), kind=kCustom, calls=%fused_computation | custom fusion | bytes 1026048 | tf_op jit(solution)/shard_map/jit(_take)/gather | solution.py:127
  14.9 0.3 copy.29
  15.2 0.1 broadcast_select_fusion
  15.3 0.0 copy-start
  15.3 2.7 %fusion.15 = (f32[500,500]{1,0:T(8,128)S(1)}, f32[4,500,500]{2,1,0:T(8,128)}) fusion(bf16[4,128,500]{1,2,0:T(8,128)(2,1)S(1)} %broadcast_select_fusion), kind=kOutput, calls=%fused_computation.32 | convolution fusion | flops 256750000 | bytes 5512000 | tf_op jit(solution)/shard_map/bki,cki->kbc/dot_general | solution.py:131
  18.0 0.0 copy-done
  18.0 0.1 copy.30
  18.2 1.3 gather_fusion.1
  19.5 0.1 copy.31
  19.6 0.4 fusion.16
  20.0 3.3 %dynamic-slice_subtract_fusion = f32[2,500,500]{2,1,0:T(8,128)} fusion(f32[4,500,500]{2,1,0:T(8,128)} %get-tuple-element.19, s32[]{:T(128)S(6)} %select_n.55, f32[500,500]{1,0:T(8,128)S(1)} %get-tuple-element.18), kind=kLoop, calls=%fused_computation.2 | loop fusion | flops 500000 | bytes 5000004 | tf_op jit(solution)/shard_map/sub | solution.py:140
  23.3 0.0 copy-start.2
  23.3 0.6 dynamic-slice_subtract_fusion.1
  23.9 0.0 all-reduce.4.cloned.1.call-update
  24.0 0.0 copy-done.2
  24.0 0.6 dynamic_slice.27.value_ref
  24.6 91.7 %all-reduce.4.cloned.1.call-done = (f32[2,500,500]{2,1,0:T(8,128)}, f32[2,500,20]{1,2,0:T(8,128)}) async-done(((f32[2,500,500]{2,1,0:T(8,128)}, f32[2,500,20]{1,2,0:T(8,128)}), (f32[2,500,500]{2,1,0:T(8,128)}, f32[2,500,20]{1,2,0:T(8,128)})) %all-reduce.4.cloned.1.call-update) | async-done | bytes 2080016 | tf_op jit(solution)/shard_map/psum | solution.py:139
  116.3 0.0 copy-start.1
  116.3 1.3 dynamic-slice_bitcast_fusion.gram_ref
  117.6 0.0 copy-done.1
  117.6 0.1 copy.32
  117.8 25.1 %shard_map.67 = bf16[500,20]{1,0:T(8,128)(2,1)S(1)} custom-call(f32[500,500]{1,0:T(8,128)S(1)} %dynamic-slice_bitcast_fusion.gram_ref, f32[500,20]{1,0:T(8,128)S(1)} %bitcast.61, f32[1]{0:T(128)} %dynamic_slice.27.value_ref), custom_call_target="tpu_custom_call" | custom-call | tf_op jit(solution)/shard_map/pallas_call | solution.py:101
  142.9 0.1 copy.33
  143.0 13.4 %all-gather.2 = bf16[4,500,20]{1,2,0:T(8,128)(2,1)S(1)} all-gather(bf16[1,500,20]{1,2,0:T(8,128)(2,1)S(1)} %copy.33), channel_id=2, replica_groups=mesh['groups'=2,'samples'=4,'blocks'=2,'folds'=2] {'samples'}, dimensions={0}, use_global_device_ids=true | all-gather | bytes 100000 | tf_op jit(solution)/shard_map/all_gather | solution.py:158
  156.4 0.2 convolution_convert_fusion
  156.6 4.5 %all-gather.1 = bf16[2,4,20,128]{3,2,1,0:T(8,128)(2,1)S(1)} all-gather(bf16[2,2,20,128]{3,2,1,0:T(8,128)(2,1)S(1)} %convolution_convert_fusion), channel_id=3, replica_groups=mesh['groups'=2,'samples'=4,'blocks'=2,'folds'=2] {'blocks'}, dimensions={1}, use_global_device_ids=true | all-gather | bytes 61440 | tf_op jit(solution)/shard_map/all_gather | solution.py:168
  161.1 0.6 copy.36
  161.7 0.2 convolution_bitcast_fusion
  161.9 0.2 fusion.9
  162.1 0.1 copy.42
  162.2 17.9 %all-reduce = (f32[2,2,20,2,2]{1,4,3,2,0:T(2,128)S(1)}, f32[2,2,20]{2,1,0:T(2,128)S(1)}) all-reduce(f32[2,2,20,2,2]{1,4,3,2,0:T(2,128)S(1)} %convolution_bitcast_fusion, f32[2,2,20]{2,1,0:T(2,128)S(1)} %bitcast.68), channel_id=1, replica_groups=mesh['groups'=2,'samples'=4,'blocks'=2,'folds'=2] {'samples'}, use_global_device_ids=true, to_apply=%region_5.6 | all-reduce | flops 400 | bytes 3200 | tf_op jit(solution)/shard_map/psum | solution.py:172
  180.1 0.7 copy.37
  180.8 0.6 multiply_bitcast_fusion.1
  (8 shorter events, 0.1 us)
Async XLA Ops:
  7.2 109.1 %all-reduce.4.cloned.1.call-start = ((), (), s32[]{:S(2)}) async-start(), calls=%async_computation | async-start | bytes 4325376 | tf_op jit(solution)/shard_map/psum | solution.py:139
  15.3 2.8 %copy-start = (bf16[20,512]{1,0:T(8,128)(2,1)S(1)}, bf16[20,512]{1,0:T(8,128)(2,1)}, u32[]{:S(2)}) copy-start(bf16[20,512]{1,0:T(8,128)(2,1)} %param.5) | copy-start | bytes 61444
  23.3 0.7 copy-start.2
  116.3 1.3 copy-start.1
Sparse Core Ops, SparseCore 0:
  24.1 92.1 all-reduce.3

commit v2 on v1

v2 whole, which is shorter than its diff:
```python
import functools

import jax
import jax.numpy as jnp
from jax import lax
from jax.experimental import pallas as pl
from jax.experimental.pallas import tpu as pltpu
from jax.sharding import PartitionSpec as P

SHRINK_LEVELS = 2
FOLDS = 4
PANEL = 128
MINI = 16


def dot_f32(a, b):
    return lax.dot_general(
        a, b, (((1,), (0,)), ((), ())), precision=lax.Precision.HIGHEST,
        preferred_element_type=jnp.float32,
    )


def sweep(block, m):
    low = m * MINI
    size = block.shape[0]
    rows = block[low:low + MINI, :]
    lane = lax.broadcasted_iota(jnp.int32, (MINI, size), 1)
    sub = lax.broadcasted_iota(jnp.int32, (MINI, size), 0)
    inside = (lane >= low) & (lane < low + MINI)
    cols = [jnp.broadcast_to(rows[:, low + j:low + j + 1], (MINI, size)) for j in range(MINI)]
    run = jnp.where(inside, jnp.where(lane - low == sub, 1.0, 0.0), rows)
    for j in range(MINI):
        inv = 1.0 / cols[j][j:j + 1, :]
        here = sub == j
        run_j = run[j:j + 1, :] * inv
        run = jnp.where(here, run_j, run - cols[j] * run_j)
        for i in range(j + 1, MINI):
            col_j = cols[i][j:j + 1, :] * inv
            cols[i] = jnp.where(here, col_j, cols[i] - cols[j] * col_j)
    lane = lax.broadcasted_iota(jnp.int32, (size, size), 1)
    sub = lax.broadcasted_iota(jnp.int32, (size, size), 0)
    in_cols = (lane >= low) & (lane < low + MINI)
    in_rows = (sub >= low) & (sub < low + MINI)
    left = jnp.where(in_cols & ~in_rows, block, 0.0)
    parts = []
    if low:
        parts.append(jnp.zeros((low, size), jnp.float32))
    parts.append(run)
    if low + MINI < size:
        parts.append(jnp.zeros((size - low - MINI, size), jnp.float32))
    placed = jnp.concatenate(parts, axis=0)
    kept = jnp.where(in_cols | in_rows, 0.0, block)
    rest = jnp.where(in_rows, placed, kept)
    return rest - dot_f32(left, placed)


def invert(work, strip):
    size = work.shape[0]

    def panel(p, carry):
        off = pl.multiple_of(p * PANEL, PANEL)
        here = pl.ds(off, PANEL)
        block = work[here, here]
        for m in range(PANEL // MINI):
            block = sweep(block, m)
        sub = lax.broadcasted_iota(jnp.int32, (size, PANEL), 0)
        col = jnp.where((sub >= off) & (sub < off + PANEL), 0.0, work[:, here])
        work[:, here] = jnp.zeros((size, PANEL), jnp.float32)
        strip[...] = dot_f32(block, work[here, :])
        strip[:, here] = block
        work[...] = work[...] - dot_f32(col, strip[...])
        work[here, :] = strip[...]
        return carry

    lax.fori_loop(0, size // PANEL, panel, 0)


def padded(count, multiple):
    return (count + multiple - 1) // multiple * multiple


def dot_nt(a, b):
    return lax.dot_general(a, b, (((1,), (1,)), ((), ())), preferred_element_type=jnp.float32)


def own_pair(total_pairs):
    place = lax.axis_index("samples") * lax.axis_size("folds") + lax.axis_index("folds")
    return lax.rem(place, total_pairs), place < total_pairs


def gather_kernel(shape, geno_ref, trait_ref, label_ref, gram_ref, held_ref, trait_own_ref,
                  stack, land, total, own_sem, next_sem, next_recv, side_sem, side_recv):
    chips, cores, variants, size, traits, part = shape
    z = lax.axis_index("samples")
    c = lax.axis_index("folds")
    width = stack.shape[1]
    rows_fold = width // FOLDS
    own_count = FOLDS // cores
    barrier = pltpu.get_barrier_semaphore()
    others = [lax.rem(c + o, cores) for o in range(1, cores)]
    has_left, has_right = z > 0, z < chips - 1

    def greet(axis, index):
        pl.semaphore_signal(barrier, inc=1, device_id={axis: index}, device_id_type=pl.DeviceIdType.MESH)

    for other in others:
        greet("folds", other)

    @pl.when(has_left)
    def _():
        greet("samples", z - 1)

    @pl.when(has_right)
    def _():
        greet("samples", z + 1)

    stack[...] = jnp.zeros_like(stack)
    stack[0:variants, :] = geno_ref[...]
    stack[size:size + traits, :] = trait_ref[...]
    label = label_ref[...]
    fold_row = lax.broadcasted_iota(jnp.int32, (16, width), 0)
    is_fold = fold_row == label
    earlier = lax.broadcasted_iota(jnp.int32, (width, width), 0) < lax.broadcasted_iota(
        jnp.int32, (width, width), 1
    )
    rank = jnp.dot(
        is_fold.astype(jnp.bfloat16), earlier.astype(jnp.bfloat16), preferred_element_type=jnp.float32
    )
    rank = jnp.sum(jnp.where(is_fold, rank, 0.0), axis=0, keepdims=True)
    target = rank + (label * rows_fold).astype(jnp.float32)
    places = lax.broadcasted_iota(jnp.int32, (width, width), 0).astype(jnp.float32)
    permute = (places == target).astype(jnp.bfloat16)
    ordered = dot_nt(stack[...], permute).astype(jnp.bfloat16)
    for q in range(FOLDS):
        for f in range(cores):
            land[z, q, f] = ordered[f * part:(f + 1) * part, q * rows_fold:(q + 1) * rows_fold]

    pl.semaphore_wait(barrier, len(others) + has_left.astype(jnp.int32) + has_right.astype(jnp.int32))

    def along(source, q, to, send):
        piece = land.at[source, q, c]
        return pltpu.make_async_remote_copy(
            src_ref=piece, dst_ref=piece, send_sem=send, recv_sem=next_recv.at[source, q],
            device_id={"samples": to}, device_id_type=pl.DeviceIdType.MESH,
        )

    def across(source, q, o):
        piece = land.at[source, q, c]
        return pltpu.make_async_remote_copy(
            src_ref=piece, dst_ref=piece, send_sem=side_sem.at[source, q, o],
            recv_sem=side_recv.at[source, q, o],
            device_id={"folds": others[o]}, device_id_type=pl.DeviceIdType.MESH,
        )

    for q in range(FOLDS):
        @pl.when(has_right)
        def _():
            along(z, q, z + 1, own_sem.at[0, q]).start()

        @pl.when(has_left)
        def _():
            along(z, q, z - 1, own_sem.at[1, q]).start()

    pair, _ = own_pair(FOLDS * SHRINK_LEVELS)
    fold = pair // SHRINK_LEVELS

    def add(source):
        columns = []
        for q in range(FOLDS):
            piece = jnp.concatenate([land[source, q, f] for f in range(cores)], axis=0)
            columns.append(jnp.where(fold == q, jnp.zeros_like(piece), piece))
        both = jnp.concatenate(columns, axis=1)
        total[...] += dot_nt(both, both[0:size, :])

    total[...] = jnp.zeros_like(total)
    add(z)

    def each_side(distance, fn):
        @pl.when(z - distance >= 0)
        def _():
            fn(z - distance, z + 1, has_right)

        @pl.when(z + distance < chips)
        def _():
            fn(z + distance, z - 1, has_left)

    def receive(distance, carry):
        for q in range(FOLDS):
            def relay(source, onward, more):
                along(source, q, z, next_sem.at[source, q]).wait_recv()

                @pl.when(more)
                def _():
                    along(source, q, onward, next_sem.at[source, q]).start()

                for o in range(cores - 1):
                    across(source, q, o).start()

            each_side(distance, relay)

        def collect(source, onward, more):
            for q in range(FOLDS):
                for o in range(cores - 1):
                    across(source, q, o).wait_recv()
            add(source)

        each_side(distance, collect)
        return carry

    lax.fori_loop(1, chips, receive, 0)
    gram_ref[...] = total[...]
    for s in range(chips):
        for f in range(cores):
            held_ref[s, f * part:(f + 1) * part, :] = land[s, fold, f]
        for k in range(own_count):
            last = jnp.concatenate([land[s, c * own_count + k, f] for f in range(cores)], axis=0)
            trait_own_ref[k, :, s * rows_fold:(s + 1) * rows_fold] = last[size:, :]

    for q in range(FOLDS):
        @pl.when(has_right)
        def _():
            along(z, q, z + 1, own_sem.at[0, q]).wait_send()

        @pl.when(has_left)
        def _():
            along(z, q, z - 1, own_sem.at[1, q]).wait_send()

    def finish(distance, carry):
        def sent(source, onward, more):
            for q in range(FOLDS):
                @pl.when(more)
                def _():
                    along(source, q, onward, next_sem.at[source, q]).wait_send()

                for o in range(cores - 1):
                    across(source, q, o).wait_send()

        each_side(distance, sent)
        return carry

    lax.fori_loop(1, chips, finish, 0)


def gather(geno, trait, label):
    chips, cores = lax.axis_size("samples"), lax.axis_size("folds")
    variants, width = geno.shape
    traits = trait.shape[0]
    size = padded(variants, PANEL)
    rows = padded(size + padded(traits, 16), 16 * cores)
    part = rows // cores
    rows_fold = width // FOLDS
    own_count = FOLDS // cores
    vmem = pl.BlockSpec(memory_space=pltpu.VMEM)
    return pl.pallas_call(
        functools.partial(gather_kernel, (chips, cores, variants, size, traits, part)),
        out_shape=(
            jax.ShapeDtypeStruct((rows, size), jnp.float32),
            jax.ShapeDtypeStruct((chips, rows, rows_fold), jnp.bfloat16),
            jax.ShapeDtypeStruct((own_count, rows - size, chips * rows_fold), jnp.bfloat16),
        ),
        in_specs=[vmem] * 3,
        out_specs=(vmem,) * 3,
        scratch_shapes=[
            pltpu.VMEM((rows, width), jnp.bfloat16),
            pltpu.VMEM((chips, FOLDS, cores, part, rows_fold), jnp.bfloat16),
            pltpu.VMEM((rows, size), jnp.float32),
            pltpu.SemaphoreType.DMA((2, FOLDS)),
            pltpu.SemaphoreType.DMA((chips, FOLDS)),
            pltpu.SemaphoreType.DMA((chips, FOLDS)),
            pltpu.SemaphoreType.DMA((chips, FOLDS, cores - 1)),
            pltpu.SemaphoreType.DMA((chips, FOLDS, cores - 1)),
        ],
        compiler_params=pltpu.CompilerParams(
            collective_id=0, has_side_effects=True, vmem_limit_bytes=48 * 1024 * 1024
        ),
    )(geno, trait, label.reshape(1, width))


def solve_kernel(variants, tally, gram_ref, held_ref, value_ref, out_ref, matrix, work, strip):
    size = work.shape[0]
    rows_fold = held_ref.shape[2]
    pair, _ = own_pair(FOLDS * SHRINK_LEVELS)
    value = value_ref[lax.rem(pair, SHRINK_LEVELS)]
    sub = lax.broadcasted_iota(jnp.int32, (size, size), 0)
    lane = lax.broadcasted_iota(jnp.int32, (size, size), 1)
    added = jnp.where(sub == lane, jnp.where(sub < variants, value, 1.0), 0.0)
    work[...] = gram_ref[0:size, :] / tally + added
    matrix[...] = work[...]
    right = gram_ref[size:, :] / tally
    invert(work, strip)
    first = dot_f32(right, work[...])
    residual = right - dot_f32(first, matrix[...])
    betas = (first + dot_f32(residual, work[...])).astype(jnp.bfloat16)
    for s in range(held_ref.shape[0]):
        preds = jnp.dot(betas, held_ref[s, 0:size, :], preferred_element_type=jnp.float32)
        out_ref[:, s * rows_fold:(s + 1) * rows_fold] = preds.astype(jnp.bfloat16)


def solve(gram, held, values, variants, tally):
    rows, size = gram.shape
    vmem = pl.BlockSpec(memory_space=pltpu.VMEM)
    return pl.pallas_call(
        functools.partial(solve_kernel, variants, tally),
        out_shape=jax.ShapeDtypeStruct((rows - size, held.shape[0] * held.shape[2]), jnp.bfloat16),
        in_specs=[vmem, vmem, pl.BlockSpec(memory_space=pltpu.SMEM)],
        out_specs=vmem,
        scratch_shapes=[
            pltpu.VMEM((size, size), jnp.float32),
            pltpu.VMEM((size, size), jnp.float32),
            pltpu.VMEM((PANEL, size), jnp.float32),
        ],
        compiler_params=pltpu.CompilerParams(vmem_limit_bytes=48 * 1024 * 1024),
    )(gram, held, values)


def exchange_kernel(shape, preds_ref, trait_ref, out_ref, gram_ref, cross_ref, slots, send_sem, recv_sem):
    chips, cores, blocks, traits = shape
    z = lax.axis_index("samples")
    c = lax.axis_index("folds")
    x = lax.axis_index("blocks")
    own_count = FOLDS // cores
    held = preds_ref.shape[1]
    rows_fold = held // chips
    pairs = FOLDS * SHRINK_LEVELS
    pair, reports = own_pair(pairs)
    fold, level = pair // SHRINK_LEVELS, lax.rem(pair, SHRINK_LEVELS)
    goal = fold // own_count
    local = lax.rem(fold, own_count)
    barrier = pltpu.get_barrier_semaphore()

    def is_self(dz, dx, dc):
        return (dz == z) & (dx == x) & (dc == c)

    senders = []
    for k in range(own_count):
        for r in range(SHRINK_LEVELS):
            place = (c * own_count + k) * SHRINK_LEVELS + r
            for b in range(blocks):
                senders.append((place // cores, b, lax.rem(place, cores), k, r))
    for sz, b, sc, k, r in senders:
        @pl.when(~is_self(sz, b, sc))
        def _():
            pl.semaphore_signal(
                barrier, inc=1, device_id={"samples": sz, "blocks": b, "folds": sc},
                device_id_type=pl.DeviceIdType.MESH,
            )

    targets = [(t, b) for t in range(chips) for b in range(blocks)]

    def message(n, t, b):
        return pltpu.make_async_remote_copy(
            src_ref=preds_ref, dst_ref=slots.at[local, x, level], send_sem=send_sem.at[n],
            recv_sem=recv_sem.at[local, x, level],
            device_id={"samples": t, "blocks": b, "folds": goal}, device_id_type=pl.DeviceIdType.MESH,
        )

    @pl.when(reports)
    def _():
        pl.semaphore_wait(barrier, len(targets) - (goal == c).astype(jnp.int32))
        for n, (t, b) in enumerate(targets):
            @pl.when(~is_self(t, b, goal))
            def _():
                message(n, t, b).start()

        @pl.when(goal == c)
        def _():
            slots[local, x, level] = preds_ref[...]

    for sz, b, sc, k, r in senders:
        @pl.when(~is_self(sz, b, sc))
        def _():
            piece = slots.at[k, b, r]
            pltpu.make_async_remote_copy(
                src_ref=piece, dst_ref=piece, send_sem=send_sem.at[0], recv_sem=recv_sem.at[k, b, r],
                device_id={"samples": sz}, device_id_type=pl.DeviceIdType.MESH,
            ).wait_recv()

    rows = slots.shape[3]
    lane = lax.broadcasted_iota(jnp.int32, (rows, gram_ref.shape[3]), 1)
    for k in range(own_count):
        trait = trait_ref[k].astype(jnp.float32)
        for r in range(SHRINK_LEVELS):
            mine = slots[k, x, r].astype(jnp.float32)
            out_ref[k, 0, r] = slots[k, x, r, 0:traits, pl.ds(pl.multiple_of(z * rows_fold, rows_fold), rows_fold)]
            block = jnp.zeros(lane.shape, jnp.float32)
            for b in range(blocks):
                for s in range(SHRINK_LEVELS):
                    theirs = slots[k, b, s].astype(jnp.float32)
                    one = jnp.sum(mine * theirs, axis=1, keepdims=True) / held
                    block = jnp.where(lane == b * SHRINK_LEVELS + s, one, block)
            gram_ref[k, r] = block
            one = jnp.sum(mine * trait, axis=1, keepdims=True) / held
            cross_ref[k, r] = jnp.where(lane == 0, one, 0.0)

    @pl.when(reports)
    def _():
        for n, (t, b) in enumerate(targets):
            @pl.when(~is_self(t, b, goal))
            def _():
                message(n, t, b).wait_send()


def exchange(preds, trait_own, traits):
    chips, cores, blocks = lax.axis_size("samples"), lax.axis_size("folds"), lax.axis_size("blocks")
    rows, held = preds.shape
    own_count = FOLDS // cores
    vmem = pl.BlockSpec(memory_space=pltpu.VMEM)
    lanes = padded(blocks * SHRINK_LEVELS, 128)
    return pl.pallas_call(
        functools.partial(exchange_kernel, (chips, cores, blocks, traits)),
        out_shape=(
            jax.ShapeDtypeStruct((own_count, 1, SHRINK_LEVELS, traits, held // chips), jnp.bfloat16),
            jax.ShapeDtypeStruct((own_count, SHRINK_LEVELS, rows, lanes), jnp.float32),
            jax.ShapeDtypeStruct((own_count, SHRINK_LEVELS, rows, lanes), jnp.float32),
        ),
        in_specs=[vmem] * 2,
        out_specs=(vmem,) * 3,
        scratch_shapes=[
            pltpu.VMEM((own_count, blocks, SHRINK_LEVELS, rows, held), jnp.bfloat16),
            pltpu.SemaphoreType.DMA((chips * blocks,)),
            pltpu.SemaphoreType.DMA((own_count, blocks, SHRINK_LEVELS)),
        ],
        compiler_params=pltpu.CompilerParams(
            collective_id=1, has_side_effects=True, vmem_limit_bytes=48 * 1024 * 1024
        ),
    )(preds, trait_own)


def per_device(allele_dosage_table, phenotype_values, individual_partition_label, shrink_strengths):
    blocks = lax.axis_size("blocks")
    variants, width = allele_dosage_table.shape
    traits = phenotype_values.shape[0]
    total_rows = lax.axis_size("samples") * width
    tally = float(total_rows - total_rows // FOLDS)
    gram, held, trait_own = gather(
        allele_dosage_table, phenotype_values, individual_partition_label
    )
    preds = solve(gram, held, shrink_strengths, variants, tally)
    predictions, level_gram, level_cross = exchange(preds, trait_own, traits)
    own_count = level_gram.shape[0]
    level_gram = level_gram[:, :, 0:traits, 0:blocks * SHRINK_LEVELS].reshape(
        own_count, 1, SHRINK_LEVELS, traits, blocks, SHRINK_LEVELS
    )
    level_cross = level_cross[:, None, :, 0:traits, 0]
    return (predictions, level_gram, level_cross)


def solution(mesh):
    in_specs = (
        P("blocks", ("groups", "samples")),
        P(None, ("groups", "samples")),
        P(("groups", "samples")),
        P(),
    )
    out_specs = (
        P("folds", "blocks", None, None, ("groups", "samples")),
        P(("groups", "folds"), "blocks", None, None, None, None),
        P(("groups", "folds"), "blocks", None, None),
    )
    return jax.shard_map(
        per_device, mesh=mesh, in_specs=in_specs, out_specs=out_specs, check_vma=False
    )
```

time: 189 us -> 62.4 us (0.33)
  waiting for transfers between devices: 91.7 us -> 0 us
  blocking collectives: 35.8 us -> 0 us
  Pallas kernels: 25.1 us -> 56 us
  between operations: 14.2 us -> 0.67 us
  other arithmetic: 9.06 us -> 0 us
  matrix products: 3.68 us -> 0 us
  local copies, waits for them, and re-layouts: 8.71 us -> 5.1 us
    psum x1 -> x0, waiting for transfers between devices: 91.7 us -> none  [per_device(): lax.psum((jnp.sum(held_gram, 0)[None] - own_gram, jnp.sum(held_cross, 0)[...]
    pallas_call x1 -> x3, Pallas kernels: 25.1 us -> 56 us  [the longest x1 24.6 us: gather(): pl.pallas_call(functools.partial(gather_kernel, (chips, cores, variants,...]
    all_gather x2 -> x0, blocking collectives: 17.9 us -> none  [the longest x1 13.4 us: per_device(): lax.all_gather(local_betas, 'samples', axis=0, tiled=True)[:pair_total]]
    psum x1 -> x0, blocking collectives: 17.9 us -> none  [per_device(): gram_sum, cross_sum = lax.psum((contrib, cross_rows), 'samples')]
    sort x1 -> x0, other arithmetic: 4.45 us -> none  [per_device(): jnp.argsort(individual_partition_label, stable=True)]
    sub x2 -> x0, other arithmetic: 3.92 us -> none  [the longest x1 3.28 us: per_device(): jnp.sum(held_gram, 0)[None] - own_gram]
    gather x4 -> x0, local copies, waits for them, and re-layouts: 3.69 us -> none  [the longest x2 2.24 us: per_device(): geno_sorted = jnp.take(allele_dosage_table, sample_order, axis=1)]
    dot_general x5 -> x0, matrix products: 3.68 us -> none  [the longest x1 2.75 us: per_device(): jnp.einsum('bki,cki->kbc', geno_sorted, geno_sorted, preferred_element_ty...]
  transfers between devices with their start and end apart: 1 -> 0, of which waited for: 1 -> 0; matrix products, arithmetic and copies ran while one was open for 0% -> 0% of each run, Pallas kernels for 0% -> 0%
where the time goes in v2:
time: 62.4 us; the launch traced here: 61.7 us
  Pallas kernels  56 us (90%)
  local copies, waits for them, and re-layouts  5.1 us (8%)
  between operations  0.67 us (1%)
    pallas_call x1, Pallas kernels, gather(): pl.pallas_call(functools.partial(gather_kernel, (chips, cores, variants,...  24.6 us
    pallas_call x1, Pallas kernels, solve(): pl.pallas_call(functools.partial(solve_kernel, variants, tally), out_shap...  22.7 us
    pallas_call x1, Pallas kernels, exchange(): pl.pallas_call(functools.partial(exchange_kernel, (chips, cores, blocks,...  8.74 us
    unnamed x9, local copies, waits for them, and re-layouts  3.72 us

profile of v2, /device:TPU:0, one launch (start us, length us, event | category | flops | bytes accessed | tf_op | source)
XLA Modules:
  0.0 61.7 jit_solution(2558498782302402577)
XLA Ops:
  0.6 0.0 copy-start
  0.6 1.0 %copy-done = bf16[500,512]{1,0:T(8,128)(2,1)S(1)} copy-done((bf16[500,512]{1,0:T(8,128)(2,1)S(1)}, bf16[500,512]{1,0:T(8,128)(2,1)}, u32[]{:S(2)}) %copy-start) | copy-done | bytes 512024
  1.7 0.0 copy-start.1
  1.7 0.7 %copy-done.1 = bf16[20,512]{1,0:T(8,128)(2,1)S(1)} copy-done((bf16[20,512]{1,0:T(8,128)(2,1)S(1)}, bf16[20,512]{1,0:T(8,128)(2,1)}, u32[]{:S(2)}) %copy-start.1) | copy-done | bytes 20504
  2.4 0.0 copy-start.2
  2.4 0.7 %copy-done.2 = s32[512]{0:T(512)S(1)} copy-done((s32[512]{0:T(512)S(1)}, s32[512]{0:T(512)}, u32[]{:S(2)}) %copy-start.2) | copy-done | bytes 2072
  3.1 24.6 %shard_map.67 = (f32[544,512]{1,0:T(8,128)S(1)}, bf16[4,544,128]{2,1,0:T(8,128)(2,1)S(1)}, bf16[2,32,512]{2,1,0:T(8,128)(2,1)S(1)}) custom-call(bf16[500,512]{1,0:T(8,128)(2,1)S(1)} %copy-done, bf16[20,512]{1,0:T(8,128)(2,1)S(1)} %copy-done.1, s32[1,512]{1,0:T(1,128)S(1)} %bitcast.7), custom_call_target="tpu_custom_call" | custom-call | tf_op jit(solution)/shard_map/pallas_call | solution.py:254
  27.7 0.0 copy-start.3
  27.7 0.6 %copy-done.3 = f32[2]{0:T(128)S(1)} copy-done((f32[2]{0:T(128)S(1)}, f32[2]{0:T(128)}, u32[]{:S(2)}) %copy-start.3) | copy-done | bytes 32
  28.3 22.7 %shard_map.68.preds_ref = bf16[32,512]{1,0:T(8,128)(2,1)S(1)} custom-call(f32[544,512]{1,0:T(8,128)S(1)} %get-tuple-element.9.gram_ref, bf16[4,544,128]{2,1,0:T(8,128)(2,1)S(1)} %get-tuple-element.10.held_ref, f32[2]{0:T(128)S(1)} %copy-done.3), custom_call_target="tpu_custom_call" | custom-call | tf_op jit(solution)/shard_map/pallas_call | solution.py:302
  51.0 8.7 %shard_map.69 = (bf16[2,1,2,20,128]{4,3,2,1,0:T(8,128)(2,1)S(1)}, f32[2,2,32,128]{3,2,1,0:T(8,128)S(1)}, f32[2,2,32,128]{3,2,1,0:T(8,128)S(1)}) custom-call(bf16[32,512]{1,0:T(8,128)(2,1)S(1)} %shard_map.68.preds_ref, bf16[2,32,512]{2,1,0:T(8,128)(2,1)S(1)} %get-tuple-element.11.trait_ref), custom_call_target="tpu_custom_call" | custom-call | tf_op jit(solution)/shard_map/pallas_call | solution.py:409
  59.7 0.6 %copy.11 = bf16[2,1,2,20,128]{4,2,3,1,0:T(2,128)(2,1)} copy(bf16[2,1,2,20,128]{4,3,2,1,0:T(8,128)(2,1)S(1)} %get-tuple-element.18) | data formatting | bytes 40960
  60.3 0.7 %slice_reduce_fusion = f32[2,2,20]{2,1,0:T(2,128)} fusion(f32[2,2,32,128]{3,2,1,0:T(8,128)S(1)} %get-tuple-element.14), kind=kLoop, calls=%fused_computation | loop fusion | bytes 640 | tf_op jit(solution)/shard_map/slice | solution.py:444
  61.0 0.7 %copy.10 = f32[2,2,20,4]{2,3,1,0:T(4,128)} copy(f32[2,2,20,4]{3,2,1,0:T(8,128)S(1)} %slice.6) | data formatting | bytes 2560 | tf_op jit(solution)/shard_map/slice | solution.py:441
  (1 shorter events, 0.0 us)
Async XLA Ops:
  0.6 1.0 %copy-start = (bf16[500,512]{1,0:T(8,128)(2,1)S(1)}, bf16[500,512]{1,0:T(8,128)(2,1)}, u32[]{:S(2)}) copy-start(bf16[500,512]{1,0:T(8,128)(2,1)} %geno_ref.1) | copy-start | bytes 1536004
  1.7 0.7 %copy-start.1 = (bf16[20,512]{1,0:T(8,128)(2,1)S(1)}, bf16[20,512]{1,0:T(8,128)(2,1)}, u32[]{:S(2)}) copy-start(bf16[20,512]{1,0:T(8,128)(2,1)} %trait_ref.1) | copy-start | bytes 61444
  2.4 0.7 %copy-start.2 = (s32[512]{0:T(512)S(1)}, s32[512]{0:T(512)}, u32[]{:S(2)}) copy-start(s32[512]{0:T(512)} %param.6) | copy-start | bytes 6148
  27.7 0.7 %copy-start.3 = (f32[2]{0:T(128)S(1)}, f32[2]{0:T(128)}, u32[]{:S(2)}) copy-start(f32[2]{0:T(128)} %value_ref.1) | copy-start | bytes 28

commit v3 on v2

--- a/solution.py
+++ b/solution.py
@@ -29,14 +29,24 @@
     inside = (lane >= low) & (lane < low + MINI)
     cols = [jnp.broadcast_to(rows[:, low + j:low + j + 1], (MINI, size)) for j in range(MINI)]
     run = jnp.where(inside, jnp.where(lane - low == sub, 1.0, 0.0), rows)
-    for j in range(MINI):
-        inv = 1.0 / cols[j][j:j + 1, :]
-        here = sub == j
-        run_j = run[j:j + 1, :] * inv
-        run = jnp.where(here, run_j, run - cols[j] * run_j)
-        for i in range(j + 1, MINI):
-            col_j = cols[i][j:j + 1, :] * inv
-            cols[i] = jnp.where(here, col_j, cols[i] - cols[j] * col_j)
+    for j in range(0, MINI, 2):
+        a, c = cols[j][j:j + 1, :], cols[j][j + 1:j + 2, :]
+        b, d = cols[j + 1][j:j + 1, :], cols[j + 1][j + 1:j + 2, :]
+        scale = 1.0 / (a * d - b * c)
+        is_first, is_second = sub == j, sub == j + 1
+        pair = is_first | is_second
+        left = jnp.where(pair, jnp.where(is_first, -1.0, 0.0), cols[j])
+        right = jnp.where(pair, jnp.where(is_first, 0.0, -1.0), cols[j + 1])
+        one = (right * c - left * d) * scale
+        two = (left * b - right * a) * scale
+
+        def eliminate(value):
+            first, second = value[j:j + 1, :], value[j + 1:j + 2, :]
+            return jnp.where(pair, 0.0, value) + (one * first + two * second)
+
+        run = eliminate(run)
+        for i in range(j + 2, MINI):
+            cols[i] = eliminate(cols[i])
     lane = lax.broadcasted_iota(jnp.int32, (size, size), 1)
     sub = lax.broadcasted_iota(jnp.int32, (size, size), 0)
     in_cols = (lane >= low) & (lane < low + MINI)

time: 62.4 us -> 63.3 us (1.014)
  Pallas kernels: 56 us -> 56.8 us
    pallas_call x1, Pallas kernels: 22.7 us -> 23.5 us  [solve(): pl.pallas_call(functools.partial(solve_kernel, variants, tally), out_shap...]
where the time goes in v3:
time: 63.3 us; the launch traced here: 62.6 us
  Pallas kernels  56.8 us (90%)
  local copies, waits for them, and re-layouts  5.1 us (8%)
  between operations  0.67 us (1%)
    pallas_call x1, Pallas kernels, gather(): pl.pallas_call(functools.partial(gather_kernel, (chips, cores, variants,...  24.6 us
    pallas_call x1, Pallas kernels, solve(): pl.pallas_call(functools.partial(solve_kernel, variants, tally), out_shap...  23.5 us
    pallas_call x1, Pallas kernels, exchange(): pl.pallas_call(functools.partial(exchange_kernel, (chips, cores, blocks,...  8.74 us
    unnamed x9, local copies, waits for them, and re-layouts  3.72 us

profile of v3, /device:TPU:0, one launch (start us, length us, event | category | flops | bytes accessed | tf_op | source)
XLA Modules:
  0.0 62.6 jit_solution(2651611312867420149)
XLA Ops:
  0.6 0.0 copy-start
  0.6 1.0 %copy-done = bf16[500,512]{1,0:T(8,128)(2,1)S(1)} copy-done((bf16[500,512]{1,0:T(8,128)(2,1)S(1)}, bf16[500,512]{1,0:T(8,128)(2,1)}, u32[]{:S(2)}) %copy-start) | copy-done | bytes 512024
  1.7 0.0 copy-start.1
  1.7 0.7 %copy-done.1 = bf16[20,512]{1,0:T(8,128)(2,1)S(1)} copy-done((bf16[20,512]{1,0:T(8,128)(2,1)S(1)}, bf16[20,512]{1,0:T(8,128)(2,1)}, u32[]{:S(2)}) %copy-start.1) | copy-done | bytes 20504
  2.4 0.0 copy-start.2
  2.4 0.7 %copy-done.2 = s32[512]{0:T(512)S(1)} copy-done((s32[512]{0:T(512)S(1)}, s32[512]{0:T(512)}, u32[]{:S(2)}) %copy-start.2) | copy-done | bytes 2072
  3.1 24.6 %shard_map.67 = (f32[544,512]{1,0:T(8,128)S(1)}, bf16[4,544,128]{2,1,0:T(8,128)(2,1)S(1)}, bf16[2,32,512]{2,1,0:T(8,128)(2,1)S(1)}) custom-call(bf16[500,512]{1,0:T(8,128)(2,1)S(1)} %copy-done, bf16[20,512]{1,0:T(8,128)(2,1)S(1)} %copy-done.1, s32[1,512]{1,0:T(1,128)S(1)} %bitcast.7), custom_call_target="tpu_custom_call" | custom-call | tf_op jit(solution)/shard_map/pallas_call | solution.py:264
  27.7 0.0 copy-start.3
  27.7 0.6 %copy-done.3 = f32[2]{0:T(128)S(1)} copy-done((f32[2]{0:T(128)S(1)}, f32[2]{0:T(128)}, u32[]{:S(2)}) %copy-start.3) | copy-done | bytes 32
  28.3 23.5 %shard_map.68.preds_ref = bf16[32,512]{1,0:T(8,128)(2,1)S(1)} custom-call(f32[544,512]{1,0:T(8,128)S(1)} %get-tuple-element.9.gram_ref, bf16[4,544,128]{2,1,0:T(8,128)(2,1)S(1)} %get-tuple-element.10.held_ref, f32[2]{0:T(128)S(1)} %copy-done.3), custom_call_target="tpu_custom_call" | custom-call | tf_op jit(solution)/shard_map/pallas_call | solution.py:312
  51.8 8.7 %shard_map.69 = (bf16[2,1,2,20,128]{4,3,2,1,0:T(8,128)(2,1)S(1)}, f32[2,2,32,128]{3,2,1,0:T(8,128)S(1)}, f32[2,2,32,128]{3,2,1,0:T(8,128)S(1)}) custom-call(bf16[32,512]{1,0:T(8,128)(2,1)S(1)} %shard_map.68.preds_ref, bf16[2,32,512]{2,1,0:T(8,128)(2,1)S(1)} %get-tuple-element.11.trait_ref), custom_call_target="tpu_custom_call" | custom-call | tf_op jit(solution)/shard_map/pallas_call | solution.py:419
  60.6 0.6 copy.11
  61.2 0.7 %slice_reduce_fusion = f32[2,2,20]{2,1,0:T(2,128)} fusion(f32[2,2,32,128]{3,2,1,0:T(8,128)S(1)} %get-tuple-element.14), kind=kLoop, calls=%fused_computation | loop fusion | bytes 640 | tf_op jit(solution)/shard_map/slice | solution.py:454
  61.9 0.7 %copy.10 = f32[2,2,20,4]{2,3,1,0:T(4,128)} copy(f32[2,2,20,4]{3,2,1,0:T(8,128)S(1)} %slice.6) | data formatting | bytes 2560 | tf_op jit(solution)/shard_map/slice | solution.py:451
  (1 shorter events, 0.0 us)
Async XLA Ops:
  0.6 1.0 %copy-start = (bf16[500,512]{1,0:T(8,128)(2,1)S(1)}, bf16[500,512]{1,0:T(8,128)(2,1)}, u32[]{:S(2)}) copy-start(bf16[500,512]{1,0:T(8,128)(2,1)} %geno_ref.1) | copy-start | bytes 1536004
  1.7 0.7 %copy-start.1 = (bf16[20,512]{1,0:T(8,128)(2,1)S(1)}, bf16[20,512]{1,0:T(8,128)(2,1)}, u32[]{:S(2)}) copy-start(bf16[20,512]{1,0:T(8,128)(2,1)} %trait_ref.1) | copy-start | bytes 61444
  2.4 0.7 %copy-start.2 = (s32[512]{0:T(512)S(1)}, s32[512]{0:T(512)}, u32[]{:S(2)}) copy-start(s32[512]{0:T(512)} %param.6) | copy-start | bytes 6148
  27.7 0.7 %copy-start.3 = (f32[2]{0:T(128)S(1)}, f32[2]{0:T(128)}, u32[]{:S(2)}) copy-start(f32[2]{0:T(128)} %value_ref.1) | copy-start | bytes 28

commit v4 on v2

--- a/solution.py
+++ b/solution.py
@@ -13,10 +13,21 @@
 MINI = 16
 
 
-def dot_f32(a, b):
+def split(a):
+    high = a.astype(jnp.bfloat16)
+    rest = a - high.astype(jnp.float32)
+    mid = rest.astype(jnp.bfloat16)
+    low = (rest - mid.astype(jnp.float32)).astype(jnp.bfloat16)
+    return high, mid, low
+
+
+def dot_f32(a, b, a_dim=1):
+    ah, am, al = split(a)
+    bh, bm, bl = split(b)
+    left = jnp.concatenate([ah, ah, am, am, ah, al], axis=a_dim)
+    right = jnp.concatenate([bh, bm, bh, bm, bl, bh], axis=0)
     return lax.dot_general(
-        a, b, (((1,), (0,)), ((), ())), precision=lax.Precision.HIGHEST,
-        preferred_element_type=jnp.float32,
+        left, right, (((a_dim,), (0,)), ((), ())), preferred_element_type=jnp.float32
     )
 
 
@@ -29,29 +40,31 @@
     inside = (lane >= low) & (lane < low + MINI)
     cols = [jnp.broadcast_to(rows[:, low + j:low + j + 1], (MINI, size)) for j in range(MINI)]
     run = jnp.where(inside, jnp.where(lane - low == sub, 1.0, 0.0), rows)
+    scale = jnp.zeros((MINI, size), jnp.float32)
     for j in range(MINI):
         inv = 1.0 / cols[j][j:j + 1, :]
         here = sub == j
-        run_j = run[j:j + 1, :] * inv
-        run = jnp.where(here, run_j, run - cols[j] * run_j)
+        scale = jnp.where(here, inv, scale)
+        ratio = jnp.where(here, 0.0, cols[j]) * inv
+        run = run - ratio * run[j:j + 1, :]
         for i in range(j + 1, MINI):
-            col_j = cols[i][j:j + 1, :] * inv
-            cols[i] = jnp.where(here, col_j, cols[i] - cols[j] * col_j)
-    lane = lax.broadcasted_iota(jnp.int32, (size, size), 1)
-    sub = lax.broadcasted_iota(jnp.int32, (size, size), 0)
-    in_cols = (lane >= low) & (lane < low + MINI)
-    in_rows = (sub >= low) & (sub < low + MINI)
-    left = jnp.where(in_cols & ~in_rows, block, 0.0)
+            cols[i] = cols[i] - ratio * cols[i][j:j + 1, :]
+    run = run * scale
+    turned = jnp.where(inside, 0.0, jnp.where(lane < low, -rows, rows))
+    update = dot_f32(turned, run, a_dim=0)
+
+    def outside(start, stop):
+        lane = lax.broadcasted_iota(jnp.int32, (stop - start, size), 1)
+        kept = jnp.where((lane >= low) & (lane < low + MINI), 0.0, block[start:stop, :])
+        return kept - update[start:stop, :]
+
     parts = []
     if low:
-        parts.append(jnp.zeros((low, size), jnp.float32))
+        parts.append(outside(0, low))
     parts.append(run)
     if low + MINI < size:
-        parts.append(jnp.zeros((size - low - MINI, size), jnp.float32))
-    placed = jnp.concatenate(parts, axis=0)
-    kept = jnp.where(in_cols | in_rows, 0.0, block)
-    rest = jnp.where(in_rows, placed, kept)
-    return rest - dot_f32(left, placed)
+        parts.append(outside(low + MINI, size))
+    return jnp.concatenate(parts, axis=0)
 
 
 def invert(work, strip):
@@ -170,7 +183,7 @@
             piece = jnp.concatenate([land[source, q, f] for f in range(cores)], axis=0)
             columns.append(jnp.where(fold == q, jnp.zeros_like(piece), piece))
         both = jnp.concatenate(columns, axis=1)
-        total[...] += dot_nt(both, both[0:size, :])
+        total[...] += dot_nt(both[0:size, :], both)
 
     total[...] = jnp.zeros_like(total)
     add(z)
@@ -254,7 +267,7 @@
     return pl.pallas_call(
         functools.partial(gather_kernel, (chips, cores, variants, size, traits, part)),
         out_shape=(
-            jax.ShapeDtypeStruct((rows, size), jnp.float32),
+            jax.ShapeDtypeStruct((size, rows), jnp.float32),
             jax.ShapeDtypeStruct((chips, rows, rows_fold), jnp.bfloat16),
             jax.ShapeDtypeStruct((own_count, rows - size, chips * rows_fold), jnp.bfloat16),
         ),
@@ -263,7 +276,7 @@
         scratch_shapes=[
             pltpu.VMEM((rows, width), jnp.bfloat16),
             pltpu.VMEM((chips, FOLDS, cores, part, rows_fold), jnp.bfloat16),
-            pltpu.VMEM((rows, size), jnp.float32),
+            pltpu.VMEM((size, rows), jnp.float32),
             pltpu.SemaphoreType.DMA((2, FOLDS)),
             pltpu.SemaphoreType.DMA((chips, FOLDS)),
             pltpu.SemaphoreType.DMA((chips, FOLDS)),
@@ -284,20 +297,22 @@
     sub = lax.broadcasted_iota(jnp.int32, (size, size), 0)
     lane = lax.broadcasted_iota(jnp.int32, (size, size), 1)
     added = jnp.where(sub == lane, jnp.where(sub < variants, value, 1.0), 0.0)
-    work[...] = gram_ref[0:size, :] / tally + added
+    work[...] = gram_ref[:, 0:size] / tally + added
     matrix[...] = work[...]
-    right = gram_ref[size:, :] / tally
+    right = gram_ref[:, size:] / tally
     invert(work, strip)
-    first = dot_f32(right, work[...])
-    residual = right - dot_f32(first, matrix[...])
-    betas = (first + dot_f32(residual, work[...])).astype(jnp.bfloat16)
+    first = dot_f32(work[...], right)
+    residual = right - dot_f32(matrix[...], first)
+    betas = (first + dot_f32(work[...], residual)).astype(jnp.bfloat16)
     for s in range(held_ref.shape[0]):
-        preds = jnp.dot(betas, held_ref[s, 0:size, :], preferred_element_type=jnp.float32)
+        preds = lax.dot_general(
+            betas, held_ref[s, 0:size, :], (((0,), (0,)), ((), ())), preferred_element_type=jnp.float32
+        )
         out_ref[:, s * rows_fold:(s + 1) * rows_fold] = preds.astype(jnp.bfloat16)
 
 
 def solve(gram, held, values, variants, tally):
-    rows, size = gram.shape
+    size, rows = gram.shape
     vmem = pl.BlockSpec(memory_space=pltpu.VMEM)
     return pl.pallas_call(
         functools.partial(solve_kernel, variants, tally),

time: 62.4 us -> 61.7 us (0.989)
  Pallas kernels: 56 us -> 55 us
    pallas_call x1, Pallas kernels: 22.7 us -> 21.8 us  [solve(): pl.pallas_call(functools.partial(solve_kernel, variants, tally), out_shap...]
where the time goes in v4:
time: 61.7 us; the launch traced here: 60.8 us
  Pallas kernels  55 us (89%)
  local copies, waits for them, and re-layouts  5.1 us (8%)
  between operations  0.67 us (1%)
    pallas_call x1, Pallas kernels, gather(): pl.pallas_call(functools.partial(gather_kernel, (chips, cores, variants,...  24.8 us
    pallas_call x1, Pallas kernels, solve(): pl.pallas_call(functools.partial(solve_kernel, variants, tally), out_shap...  21.8 us
    pallas_call x1, Pallas kernels, exchange(): pl.pallas_call(functools.partial(exchange_kernel, (chips, cores, blocks,...  8.37 us
    unnamed x9, local copies, waits for them, and re-layouts  3.72 us

profile of v4, /device:TPU:0, one launch (start us, length us, event | category | flops | bytes accessed | tf_op | source)
XLA Modules:
  0.0 60.8 jit_solution(15733295663921321679)
XLA Ops:
  0.6 0.0 copy-start
  0.6 1.0 %copy-done = bf16[500,512]{1,0:T(8,128)(2,1)S(1)} copy-done((bf16[500,512]{1,0:T(8,128)(2,1)S(1)}, bf16[500,512]{1,0:T(8,128)(2,1)}, u32[]{:S(2)}) %copy-start) | copy-done | bytes 512024
  1.7 0.0 copy-start.1
  1.7 0.7 %copy-done.1 = bf16[20,512]{1,0:T(8,128)(2,1)S(1)} copy-done((bf16[20,512]{1,0:T(8,128)(2,1)S(1)}, bf16[20,512]{1,0:T(8,128)(2,1)}, u32[]{:S(2)}) %copy-start.1) | copy-done | bytes 20504
  2.4 0.0 copy-start.2
  2.4 0.7 %copy-done.2 = s32[512]{0:T(512)S(1)} copy-done((s32[512]{0:T(512)S(1)}, s32[512]{0:T(512)}, u32[]{:S(2)}) %copy-start.2) | copy-done | bytes 2072
  3.1 24.8 %shard_map.67 = (f32[512,544]{1,0:T(8,128)S(1)}, bf16[4,544,128]{2,1,0:T(8,128)(2,1)S(1)}, bf16[2,32,512]{2,1,0:T(8,128)(2,1)S(1)}) custom-call(bf16[500,512]{1,0:T(8,128)(2,1)S(1)} %copy-done, bf16[20,512]{1,0:T(8,128)(2,1)S(1)} %copy-done.1, s32[1,512]{1,0:T(1,128)S(1)} %bitcast.7), custom_call_target="tpu_custom_call" | custom-call | tf_op jit(solution)/shard_map/pallas_call | solution.py:267
  27.9 0.0 copy-start.3
  27.9 0.6 %copy-done.3 = f32[2]{0:T(128)S(1)} copy-done((f32[2]{0:T(128)S(1)}, f32[2]{0:T(128)}, u32[]{:S(2)}) %copy-start.3) | copy-done | bytes 32
  28.6 21.8 %shard_map.68.preds_ref = bf16[32,512]{1,0:T(8,128)(2,1)S(1)} custom-call(f32[512,544]{1,0:T(8,128)S(1)} %get-tuple-element.9.gram_ref, bf16[4,544,128]{2,1,0:T(8,128)(2,1)S(1)} %get-tuple-element.10.held_ref, f32[2]{0:T(128)S(1)} %copy-done.3), custom_call_target="tpu_custom_call" | custom-call | tf_op jit(solution)/shard_map/pallas_call | solution.py:317
  50.4 8.4 %shard_map.69 = (bf16[2,1,2,20,128]{4,3,2,1,0:T(8,128)(2,1)S(1)}, f32[2,2,32,128]{3,2,1,0:T(8,128)S(1)}, f32[2,2,32,128]{3,2,1,0:T(8,128)S(1)}) custom-call(bf16[32,512]{1,0:T(8,128)(2,1)S(1)} %shard_map.68.preds_ref, bf16[2,32,512]{2,1,0:T(8,128)(2,1)S(1)} %get-tuple-element.11.trait_ref), custom_call_target="tpu_custom_call" | custom-call | tf_op jit(solution)/shard_map/pallas_call | solution.py:424
  58.8 0.6 %copy.11 = bf16[2,1,2,20,128]{4,2,3,1,0:T(2,128)(2,1)} copy(bf16[2,1,2,20,128]{4,3,2,1,0:T(8,128)(2,1)S(1)} %get-tuple-element.18) | data formatting | bytes 40960
  59.4 0.7 %slice_reduce_fusion = f32[2,2,20]{2,1,0:T(2,128)} fusion(f32[2,2,32,128]{3,2,1,0:T(8,128)S(1)} %get-tuple-element.14), kind=kLoop, calls=%fused_computation | loop fusion | bytes 640 | tf_op jit(solution)/shard_map/slice | solution.py:459
  60.1 0.7 %copy.10 = f32[2,2,20,4]{2,3,1,0:T(4,128)} copy(f32[2,2,20,4]{3,2,1,0:T(8,128)S(1)} %slice.6) | data formatting | bytes 2560 | tf_op jit(solution)/shard_map/slice | solution.py:456
  (1 shorter events, 0.0 us)
Async XLA Ops:
  0.6 1.0 %copy-start = (bf16[500,512]{1,0:T(8,128)(2,1)S(1)}, bf16[500,512]{1,0:T(8,128)(2,1)}, u32[]{:S(2)}) copy-start(bf16[500,512]{1,0:T(8,128)(2,1)} %geno_ref.1) | copy-start | bytes 1536004
  1.7 0.7 %copy-start.1 = (bf16[20,512]{1,0:T(8,128)(2,1)S(1)}, bf16[20,512]{1,0:T(8,128)(2,1)}, u32[]{:S(2)}) copy-start(bf16[20,512]{1,0:T(8,128)(2,1)} %trait_ref.1) | copy-start | bytes 61444
  2.4 0.7 %copy-start.2 = (s32[512]{0:T(512)S(1)}, s32[512]{0:T(512)}, u32[]{:S(2)}) copy-start(s32[512]{0:T(512)} %param.6) | copy-start | bytes 6148
  27.9 0.7 %copy-start.3 = (f32[2]{0:T(128)S(1)}, f32[2]{0:T(128)}, u32[]{:S(2)}) copy-start(f32[2]{0:T(128)} %value_ref.1) | copy-start | bytes 28

commit v5 on v4

v5 whole, which is shorter than its diff:
```python
import functools

import jax
import jax.numpy as jnp
from jax import lax
from jax.experimental import pallas as pl
from jax.experimental.pallas import tpu as pltpu
from jax.sharding import PartitionSpec as P

SHRINK_LEVELS = 2
FOLDS = 4
PANEL = 128
MINI = 16


def split(a):
    high = a.astype(jnp.bfloat16)
    rest = a - high.astype(jnp.float32)
    mid = rest.astype(jnp.bfloat16)
    low = (rest - mid.astype(jnp.float32)).astype(jnp.bfloat16)
    return high, mid, low


def dot_f32(a, b, a_dim=1):
    ah, am, al = split(a)
    bh, bm, bl = split(b)
    left = jnp.concatenate([ah, ah, am, am, ah, al], axis=a_dim)
    right = jnp.concatenate([bh, bm, bh, bm, bl, bh], axis=0)
    return lax.dot_general(
        left, right, (((a_dim,), (0,)), ((), ())), preferred_element_type=jnp.float32
    )


def sweep(block, m):
    low = m * MINI
    size = block.shape[0]
    rows = block[low:low + MINI, :]
    lane = lax.broadcasted_iota(jnp.int32, (MINI, size), 1)
    sub = lax.broadcasted_iota(jnp.int32, (MINI, size), 0)
    inside = (lane >= low) & (lane < low + MINI)
    cols = [jnp.broadcast_to(rows[:, low + j:low + j + 1], (MINI, size)) for j in range(MINI)]
    run = jnp.where(inside, jnp.where(lane - low == sub, 1.0, 0.0), rows)
    scale = jnp.zeros((MINI, size), jnp.float32)
    for j in range(MINI):
        inv = 1.0 / cols[j][j:j + 1, :]
        here = sub == j
        scale = jnp.where(here, inv, scale)
        ratio = jnp.where(here, 0.0, cols[j]) * inv
        run = run - ratio * run[j:j + 1, :]
        for i in range(j + 1, MINI):
            cols[i] = cols[i] - ratio * cols[i][j:j + 1, :]
    run = run * scale
    turned = jnp.where(inside, 0.0, jnp.where(lane < low, -rows, rows))
    update = dot_f32(turned, run, a_dim=0)

    def outside(start, stop):
        lane = lax.broadcasted_iota(jnp.int32, (stop - start, size), 1)
        kept = jnp.where((lane >= low) & (lane < low + MINI), 0.0, block[start:stop, :])
        return kept - update[start:stop, :]

    parts = []
    if low:
        parts.append(outside(0, low))
    parts.append(run)
    if low + MINI < size:
        parts.append(outside(low + MINI, size))
    return jnp.concatenate(parts, axis=0)


def invert(work, strip, during):
    size = work.shape[0]

    def panel(p, carry):
        @pl.when(p == size // PANEL - 1)
        def _():
            during()

        off = pl.multiple_of(p * PANEL, PANEL)
        here = pl.ds(off, PANEL)
        block = work[here, here]
        for m in range(PANEL // MINI):
            block = sweep(block, m)
        sub = lax.broadcasted_iota(jnp.int32, (size, PANEL), 0)
        col = jnp.where((sub >= off) & (sub < off + PANEL), 0.0, work[:, here])
        work[:, here] = jnp.zeros((size, PANEL), jnp.float32)
        strip[...] = dot_f32(block, work[here, :])
        strip[:, here] = block
        work[...] = work[...] - dot_f32(col, strip[...])
        work[here, :] = strip[...]
        return carry

    lax.fori_loop(0, size // PANEL, panel, 0)


def padded(count, multiple):
    return (count + multiple - 1) // multiple * multiple


def dot_nt(a, b):
    return lax.dot_general(a, b, (((1,), (1,)), ((), ())), preferred_element_type=jnp.float32)


def own_pair(total_pairs):
    place = lax.axis_index("samples") * lax.axis_size("folds") + lax.axis_index("folds")
    return lax.rem(place, total_pairs), place < total_pairs


def kernel(shape, geno_hbm, trait_hbm, label_hbm, value_ref, out_ref, gram_ref, cross_ref,
           geno_ref, trait_ref, label_ref, stack, land, total, work, strip, preds_ref, slots,
           load_sem, own_sem, next_sem, next_recv, side_sem, side_recv, send_sem, recv_sem):
    chips, cores, blocks, variants, size, traits, part = shape
    z = lax.axis_index("samples")
    c = lax.axis_index("folds")
    x = lax.axis_index("blocks")
    width = stack.shape[1]
    rows_fold = width // FOLDS
    held = chips * rows_fold
    tally = chips * width - held
    own_count = FOLDS // cores
    pairs = FOLDS * SHRINK_LEVELS
    pair, reports = own_pair(pairs)
    fold, level = pair // SHRINK_LEVELS, lax.rem(pair, SHRINK_LEVELS)
    goal = fold // own_count
    local = lax.rem(fold, own_count)
    others = [lax.rem(c + o, cores) for o in range(1, cores)]
    has_left, has_right = z > 0, z < chips - 1
    last_right = ((chips - 1) * cores % pairs) // SHRINK_LEVELS
    last_left = 0
    early_right = [q for q in range(FOLDS) if q != last_right]
    early_left = [q for q in range(FOLDS) if q != last_left]

    loads = [
        pltpu.make_async_copy(source, goal_ref, load_sem.at[n])
        for n, (source, goal_ref) in enumerate(
            [(label_hbm, label_ref), (geno_hbm, geno_ref), (trait_hbm, trait_ref)]
        )
    ]
    for load in loads:
        load.start()

    barrier = pltpu.get_barrier_semaphore()

    def greet(**place):
        pl.semaphore_signal(barrier, inc=1, device_id=place, device_id_type=pl.DeviceIdType.MESH)

    for other in others:
        greet(folds=other)

    @pl.when(has_left)
    def _():
        greet(samples=z - 1)

    @pl.when(has_right)
    def _():
        greet(samples=z + 1)

    def is_self(dz, dx, dc):
        return (dz == z) & (dx == x) & (dc == c)

    senders = []
    for k in range(own_count):
        for r in range(SHRINK_LEVELS):
            place = (c * own_count + k) * SHRINK_LEVELS + r
            for b in range(blocks):
                senders.append((place // cores, b, lax.rem(place, cores), k, r))
    for sz, b, sc, k, r in senders:
        @pl.when(~is_self(sz, b, sc))
        def _():
            greet(samples=sz, blocks=b, folds=sc)

    targets = [(t, b) for t in range(chips) for b in range(blocks)]

    stack[...] = jnp.zeros_like(stack)
    total[...] = jnp.zeros_like(total)
    for load in loads:
        load.wait()
    stack[0:variants, :] = geno_ref[...]
    stack[size:size + traits, :] = trait_ref[...]
    label = label_ref[...]
    fold_row = lax.broadcasted_iota(jnp.int32, (16, width), 0)
    is_fold = fold_row == label
    earlier = lax.broadcasted_iota(jnp.int32, (width, width), 0) < lax.broadcasted_iota(
        jnp.int32, (width, width), 1
    )
    rank = jnp.dot(
        is_fold.astype(jnp.bfloat16), earlier.astype(jnp.bfloat16), preferred_element_type=jnp.float32
    )
    rank = jnp.sum(jnp.where(is_fold, rank, 0.0), axis=0, keepdims=True)
    target = rank + (label * rows_fold).astype(jnp.float32)
    places = lax.broadcasted_iota(jnp.int32, (width, width), 0).astype(jnp.float32)
    permute = (places == target).astype(jnp.bfloat16)
    ordered = dot_nt(stack[...], permute).astype(jnp.bfloat16)
    for q in range(FOLDS):
        for f in range(cores):
            land[z, q, f] = ordered[f * part:(f + 1) * part, q * rows_fold:(q + 1) * rows_fold]

    expected = len(others) + has_left.astype(jnp.int32) + has_right.astype(jnp.int32)
    farther = len(targets) - (goal == c).astype(jnp.int32)
    pl.semaphore_wait(barrier, expected + jnp.where(reports, farther, 0))

    def along(source, q, to, send):
        piece = land.at[source, q, c]
        return pltpu.make_async_remote_copy(
            src_ref=piece, dst_ref=piece, send_sem=send, recv_sem=next_recv.at[source, q],
            device_id={"samples": to}, device_id_type=pl.DeviceIdType.MESH,
        )

    def across(source, q, o):
        piece = land.at[source, q, c]
        return pltpu.make_async_remote_copy(
            src_ref=piece, dst_ref=piece, send_sem=side_sem.at[source, q, o],
            recv_sem=side_recv.at[source, q, o],
            device_id={"folds": others[o]}, device_id_type=pl.DeviceIdType.MESH,
        )

    def own_chunk(q, to_right):
        n, to = (0, z + 1) if to_right else (1, z - 1)
        return along(z, q, to, own_sem.at[n, q])

    for q_right, q_left in zip(early_right, early_left):
        @pl.when(has_right)
        def _():
            own_chunk(q_right, True).start()

        @pl.when(has_left)
        def _():
            own_chunk(q_left, False).start()

    def add(source, chunks):
        columns = []
        for q in chunks:
            piece = jnp.concatenate([land[source, q, f] for f in range(cores)], axis=0)
            columns.append(jnp.where(fold == q, jnp.zeros_like(piece), piece))
        both = jnp.concatenate(columns, axis=1)
        total[...] += dot_nt(both[0:size, :], both)

    add(z, range(FOLDS))

    def each_side(distance, fn):
        @pl.when(z - distance >= 0)
        def _():
            fn(z - distance, z + 1, has_right, early_right, last_right)

        @pl.when(z + distance < chips)
        def _():
            fn(z + distance, z - 1, has_left, early_left, last_left)

    def pass_on(source, q, onward, more):
        along(source, q, z, next_sem.at[source, q]).wait_recv()

        @pl.when(more)
        def _():
            along(source, q, onward, next_sem.at[source, q]).start()

        for o in range(cores - 1):
            across(source, q, o).start()

    def receive(distance, carry):
        for n in range(FOLDS - 1):
            each_side(distance, lambda source, onward, more, early, last: pass_on(source, early[n], onward, more))

        def collect(source, onward, more, early, last):
            for q in early:
                for o in range(cores - 1):
                    across(source, q, o).wait_recv()
            add(source, early)

        each_side(distance, collect)
        return carry

    lax.fori_loop(1, chips, receive, 0)

    @pl.when(has_right)
    def _():
        own_chunk(last_right, True).start()

    @pl.when(has_left)
    def _():
        own_chunk(last_left, False).start()

    def idle(more, last):
        return ~more & (fold == last)

    def receive_last(distance, carry):
        def relay(source, onward, more, early, last):
            @pl.when(~idle(more, last))
            def _():
                pass_on(source, last, onward, more)

        each_side(distance, relay)
        return carry

    def collect_last(distance, carry):
        def collect(source, onward, more, early, last):
            @pl.when(~idle(more, last))
            def _():
                for o in range(cores - 1):
                    across(source, last, o).wait_recv()
                add(source, [last])

        each_side(distance, collect)
        return carry

    lax.fori_loop(1, chips, receive_last, 0)
    lax.fori_loop(1, chips, collect_last, 0)

    def late():
        def step(distance, carry):
            def relay(source, onward, more, early, last):
                @pl.when(idle(more, last))
                def _():
                    pass_on(source, last, onward, more)

            each_side(distance, relay)
            return carry

        lax.fori_loop(1, chips, step, 0)

    sub = lax.broadcasted_iota(jnp.int32, (size, size), 0)
    lane = lax.broadcasted_iota(jnp.int32, (size, size), 1)
    value = jnp.where(level == 0, value_ref[0], value_ref[SHRINK_LEVELS - 1])
    for r in range(1, SHRINK_LEVELS - 1):
        value = jnp.where(level == r, value_ref[r], value)
    added = jnp.where(sub == lane, jnp.where(sub < variants, value, 1.0), 0.0)
    total[...] = total[...] * (1.0 / tally)
    total[:, 0:size] = total[:, 0:size] + added
    work[...] = total[:, 0:size]
    invert(work, strip, late)
    right = total[:, size:]
    first = dot_f32(work[...], right)
    residual = right - dot_f32(total[:, 0:size], first)
    betas = (first + dot_f32(work[...], residual)).astype(jnp.bfloat16)

    def late_done(distance, carry):
        def wait(source, onward, more, early, last):
            @pl.when(idle(more, last))
            def _():
                for o in range(cores - 1):
                    across(source, last, o).wait_recv()

        each_side(distance, wait)
        return carry

    lax.fori_loop(1, chips, late_done, 0)
    for s in range(chips):
        chunk = jnp.concatenate([land[s, fold, f] for f in range(cores)], axis=0)
        preds = lax.dot_general(
            betas, chunk[0:size, :], (((0,), (0,)), ((), ())), preferred_element_type=jnp.float32
        )
        preds_ref[:, s * rows_fold:(s + 1) * rows_fold] = preds.astype(jnp.bfloat16)

    def message(n, t, b):
        return pltpu.make_async_remote_copy(
            src_ref=preds_ref, dst_ref=slots.at[local, x, level], send_sem=send_sem.at[n],
            recv_sem=recv_sem.at[local, x, level],
            device_id={"samples": t, "blocks": b, "folds": goal}, device_id_type=pl.DeviceIdType.MESH,
        )

    @pl.when(reports)
    def _():
        for n, (t, b) in enumerate(targets):
            @pl.when(~is_self(t, b, goal))
            def _():
                message(n, t, b).start()

        @pl.when(goal == c)
        def _():
            slots[local, x, level] = preds_ref[...]

    for sz, b, sc, k, r in senders:
        @pl.when(~is_self(sz, b, sc))
        def _():
            piece = slots.at[k, b, r]
            pltpu.make_async_remote_copy(
                src_ref=piece, dst_ref=piece, send_sem=send_sem.at[0], recv_sem=recv_sem.at[k, b, r],
                device_id={"samples": sz}, device_id_type=pl.DeviceIdType.MESH,
            ).wait_recv()

    rows = slots.shape[3]
    lane = lax.broadcasted_iota(jnp.int32, (rows, gram_ref.shape[3]), 1)
    for k in range(own_count):
        pieces = []
        for s in range(chips):
            chunk = jnp.concatenate([land[s, c * own_count + k, f] for f in range(cores)], axis=0)
            pieces.append(chunk[size:, :])
        trait = jnp.concatenate(pieces, axis=1).astype(jnp.float32)
        for r in range(SHRINK_LEVELS):
            mine = slots[k, x, r].astype(jnp.float32)
            out_ref[k, 0, r] = slots[k, x, r, 0:traits, pl.ds(pl.multiple_of(z * rows_fold, rows_fold), rows_fold)]
            block = jnp.zeros(lane.shape, jnp.float32)
            for b in range(blocks):
                for s in range(SHRINK_LEVELS):
                    theirs = slots[k, b, s].astype(jnp.float32)
                    one = jnp.sum(mine * theirs, axis=1, keepdims=True) / held
                    block = jnp.where(lane == b * SHRINK_LEVELS + s, one, block)
            gram_ref[k, r] = block
            one = jnp.sum(mine * trait, axis=1, keepdims=True) / held
            cross_ref[k, r] = jnp.where(lane == 0, one, 0.0)

    @pl.when(reports)
    def _():
        for n, (t, b) in enumerate(targets):
            @pl.when(~is_self(t, b, goal))
            def _():
                message(n, t, b).wait_send()

    for q in range(FOLDS):
        @pl.when(has_right)
        def _():
            own_chunk(q, True).wait_send()

        @pl.when(has_left)
        def _():
            own_chunk(q, False).wait_send()

    def finish(distance, carry):
        def sent(source, onward, more, early, last):
            for q in range(FOLDS):
                @pl.when(more)
                def _():
                    along(source, q, onward, next_sem.at[source, q]).wait_send()

                for o in range(cores - 1):
                    across(source, q, o).wait_send()

        each_side(distance, sent)
        return carry

    lax.fori_loop(1, chips, finish, 0)


def per_device(allele_dosage_table, phenotype_values, individual_partition_label, shrink_strengths):
    chips, cores, blocks = lax.axis_size("samples"), lax.axis_size("folds"), lax.axis_size("blocks")
    variants, width = allele_dosage_table.shape
    traits = phenotype_values.shape[0]
    size = padded(variants, PANEL)
    rows = padded(size + padded(traits, 16), 16 * cores)
    part = rows // cores
    rows_fold = width // FOLDS
    held = chips * rows_fold
    own_count = FOLDS // cores
    lanes = padded(blocks * SHRINK_LEVELS, 128)
    vmem = pl.BlockSpec(memory_space=pltpu.VMEM)
    hbm = pl.BlockSpec(memory_space=pl.ANY)
    predictions, level_gram, level_cross = pl.pallas_call(
        functools.partial(kernel, (chips, cores, blocks, variants, size, traits, part)),
        out_shape=(
            jax.ShapeDtypeStruct((own_count, 1, SHRINK_LEVELS, traits, rows_fold), jnp.bfloat16),
            jax.ShapeDtypeStruct((own_count, SHRINK_LEVELS, rows - size, lanes), jnp.float32),
            jax.ShapeDtypeStruct((own_count, SHRINK_LEVELS, rows - size, lanes), jnp.float32),
        ),
        in_specs=[hbm, hbm, hbm, pl.BlockSpec(memory_space=pltpu.SMEM)],
        out_specs=(vmem,) * 3,
        scratch_shapes=[
            pltpu.VMEM((variants, width), jnp.bfloat16),
            pltpu.VMEM((traits, width), jnp.bfloat16),
            pltpu.VMEM((1, width), jnp.int32),
            pltpu.VMEM((rows, width), jnp.bfloat16),
            pltpu.VMEM((chips, FOLDS, cores, part, rows_fold), jnp.bfloat16),
            pltpu.VMEM((size, rows), jnp.float32),
            pltpu.VMEM((size, size), jnp.float32),
            pltpu.VMEM((PANEL, size), jnp.float32),
            pltpu.VMEM((rows - size, held), jnp.bfloat16),
            pltpu.VMEM((own_count, blocks, SHRINK_LEVELS, rows - size, held), jnp.bfloat16),
            pltpu.SemaphoreType.DMA((3,)),
            pltpu.SemaphoreType.DMA((2, FOLDS)),
            pltpu.SemaphoreType.DMA((chips, FOLDS)),
            pltpu.SemaphoreType.DMA((chips, FOLDS)),
            pltpu.SemaphoreType.DMA((chips, FOLDS, cores - 1)),
            pltpu.SemaphoreType.DMA((chips, FOLDS, cores - 1)),
            pltpu.SemaphoreType.DMA((chips * blocks,)),
            pltpu.SemaphoreType.DMA((own_count, blocks, SHRINK_LEVELS)),
        ],
        compiler_params=pltpu.CompilerParams(
            collective_id=0, has_side_effects=True, vmem_limit_bytes=60 * 1024 * 1024
        ),
    )(allele_dosage_table, phenotype_values, individual_partition_label.reshape(1, width), shrink_strengths)
    level_gram = level_gram[:, :, 0:traits, 0:blocks * SHRINK_LEVELS].reshape(
        own_count, 1, SHRINK_LEVELS, traits, blocks, SHRINK_LEVELS
    )
    level_cross = level_cross[:, None, :, 0:traits, 0]
    return (predictions, level_gram, level_cross)


def solution(mesh):
    in_specs = (
        P("blocks", ("groups", "samples")),
        P(None, ("groups", "samples")),
        P(("groups", "samples")),
        P(),
    )
    out_specs = (
        P("folds", "blocks", None, None, ("groups", "samples")),
        P(("groups", "folds"), "blocks", None, None, None, None),
        P(("groups", "folds"), "blocks", None, None),
    )
    return jax.shard_map(
        per_device, mesh=mesh, in_specs=in_specs, out_specs=out_specs, check_vma=False
    )
```

time: 61.7 us -> 63.8 us (1.034); the launches traced: 60.8 us -> 63.5 us
  Pallas kernels: 55 us -> 59.3 us
  local copies, waits for them, and re-layouts: 5.1 us -> 3.57 us
    pallas_call x3 -> x1, Pallas kernels: 55 us -> 59.3 us  [per_device(): pl.pallas_call(functools.partial(kernel, (chips, cores, blocks, variants,...]
    unnamed x9 -> x3, local copies, waits for them, and re-layouts: 3.72 us -> 1.4 us
    slice x1, local copies, waits for them, and re-layouts: 0.67 us -> 1.47 us  [per_device(): level_cross = level_cross[:, None, :, 0:traits, 0]]
where the time goes in v5:
time: 63.8 us; the launch traced here: 63.5 us
  Pallas kernels  59.3 us (93%)
  local copies, waits for them, and re-layouts  3.57 us (6%)
  between operations  0.65 us (1%)
    pallas_call x1, Pallas kernels, per_device(): pl.pallas_call(functools.partial(kernel, (chips, cores, blocks, variants,...  59.3 us
    slice x1, local copies, waits for them, and re-layouts, per_device(): level_cross = level_cross[:, None, :, 0:traits, 0]  1.47 us
    unnamed x3, local copies, waits for them, and re-layouts  1.4 us

profile of v5, /device:TPU:0, one launch (start us, length us, event | category | flops | bytes accessed | tf_op | source)
XLA Modules:
  0.0 63.5 jit_solution(2907402344937620794)
XLA Ops:
  0.6 59.3 %shard_map.67 = (bf16[2,1,2,20,128]{4,3,2,1,0:T(8,128)(2,1)}, f32[2,2,32,128]{3,2,1,0:T(8,128)}, f32[2,2,32,128]{3,2,1,0:T(8,128)}) custom-call(bf16[500,512]{1,0:T(8,128)(2,1)} %geno_hbm.1, bf16[20,512]{1,0:T(8,128)(2,1)} %trait_hbm.1, s32[1,512]{1,0:T(1,128)} %bitcast.8, f32[2]{0:T(128)} %value_ref.1), custom_call_target="tpu_custom_call" | custom-call | tf_op jit(solution)/shard_map/pallas_call | solution.py:445
  60.0 0.0 copy-start
  60.0 1.4 %copy.11 = bf16[2,1,2,20,128]{4,2,3,1,0:T(2,128)(2,1)} copy(bf16[2,1,2,20,128]{4,3,2,1,0:T(8,128)(2,1)} %get-tuple-element.12) | data formatting | bytes 40960
  61.4 1.5 %slice_reduce_fusion = f32[2,2,20]{2,1,0:T(2,128)} fusion(f32[2,2,32,128]{3,2,1,0:T(8,128)} %get-tuple-element.8), kind=kLoop, calls=%fused_computation | loop fusion | bytes 640 | tf_op jit(solution)/shard_map/slice | solution.py:481
  62.8 0.0 copy-done
  62.8 0.7 %copy.10 = f32[2,2,20,4]{2,3,1,0:T(4,128)} copy(f32[2,2,20,4]{3,2,1,0:T(8,128)S(1)} %slice.6) | data formatting | bytes 2560 | tf_op jit(solution)/shard_map/slice | solution.py:478
  (1 shorter events, 0.0 us)
Async XLA Ops:
  60.0 2.9 %copy-start = (f32[2,2,32,128]{3,2,1,0:T(8,128)S(1)}, f32[2,2,32,128]{3,2,1,0:T(8,128)}, u32[]{:S(2)}) copy-start(f32[2,2,32,128]{3,2,1,0:T(8,128)} %get-tuple-element.7) | copy-start | bytes 196612

commit v6 on v5

--- a/solution.py
+++ b/solution.py
@@ -255,28 +255,39 @@
         for o in range(cores - 1):
             across(source, q, o).start()
 
+    def collect(source, onward, more, early, last):
+        for q in early:
+            for o in range(cores - 1):
+                across(source, q, o).wait_recv()
+        add(source, early)
+
     def receive(distance, carry):
         for n in range(FOLDS - 1):
             each_side(distance, lambda source, onward, more, early, last: pass_on(source, early[n], onward, more))
 
-        def collect(source, onward, more, early, last):
-            for q in early:
-                for o in range(cores - 1):
-                    across(source, q, o).wait_recv()
-            add(source, early)
-
-        each_side(distance, collect)
+        @pl.when((z == distance) & has_right)
+        def _():
+            own_chunk(last_right, True).start()
+
+        @pl.when((z + distance == chips - 1) & has_left)
+        def _():
+            own_chunk(last_left, False).start()
+
+        @pl.when(distance > 1)
+        def _():
+            each_side(distance - 1, collect)
+
         return carry
 
-    lax.fori_loop(1, chips, receive, 0)
-
-    @pl.when(has_right)
+    @pl.when(~has_left & has_right)
     def _():
         own_chunk(last_right, True).start()
 
-    @pl.when(has_left)
+    @pl.when(~has_right & has_left)
     def _():
         own_chunk(last_left, False).start()
+
+    lax.fori_loop(1, chips, receive, 0)
 
     def idle(more, last):
         return ~more & (fold == last)
@@ -291,17 +302,19 @@
         return carry
 
     def collect_last(distance, carry):
-        def collect(source, onward, more, early, last):
+        def collect_one(source, onward, more, early, last):
             @pl.when(~idle(more, last))
             def _():
                 for o in range(cores - 1):
                     across(source, last, o).wait_recv()
                 add(source, [last])
 
-        each_side(distance, collect)
+        each_side(distance, collect_one)
         return carry
 
     lax.fori_loop(1, chips, receive_last, 0)
+    if chips > 1:
+        each_side(chips - 1, collect)
     lax.fori_loop(1, chips, collect_last, 0)
 
     def late():
@@ -377,25 +390,27 @@
             ).wait_recv()
 
     rows = slots.shape[3]
-    lane = lax.broadcasted_iota(jnp.int32, (rows, gram_ref.shape[3]), 1)
+
+    def same_trait(mine, theirs):
+        found = dot_nt(mine, theirs)
+        at = lax.broadcasted_iota(jnp.int32, found.shape, 0)
+        other = lax.rem(lax.broadcasted_iota(jnp.int32, found.shape, 1), rows)
+        return jnp.sum(jnp.where(at == other, found, 0.0), axis=0, keepdims=True) / held
+
     for k in range(own_count):
         pieces = []
         for s in range(chips):
             chunk = jnp.concatenate([land[s, c * own_count + k, f] for f in range(cores)], axis=0)
             pieces.append(chunk[size:, :])
-        trait = jnp.concatenate(pieces, axis=1).astype(jnp.float32)
+        trait = jnp.concatenate(pieces, axis=1)
+        everything = jnp.concatenate(
+            [slots[k, b, s] for b in range(blocks) for s in range(SHRINK_LEVELS)], axis=0
+        )
         for r in range(SHRINK_LEVELS):
-            mine = slots[k, x, r].astype(jnp.float32)
+            mine = slots[k, x, r]
             out_ref[k, 0, r] = slots[k, x, r, 0:traits, pl.ds(pl.multiple_of(z * rows_fold, rows_fold), rows_fold)]
-            block = jnp.zeros(lane.shape, jnp.float32)
-            for b in range(blocks):
-                for s in range(SHRINK_LEVELS):
-                    theirs = slots[k, b, s].astype(jnp.float32)
-                    one = jnp.sum(mine * theirs, axis=1, keepdims=True) / held
-                    block = jnp.where(lane == b * SHRINK_LEVELS + s, one, block)
-            gram_ref[k, r] = block
-            one = jnp.sum(mine * trait, axis=1, keepdims=True) / held
-            cross_ref[k, r] = jnp.where(lane == 0, one, 0.0)
+            gram_ref[k, r] = same_trait(mine, everything)
+            cross_ref[k, r] = same_trait(mine, trait)
 
     @pl.when(reports)
     def _():
@@ -439,15 +454,16 @@
     rows_fold = width // FOLDS
     held = chips * rows_fold
     own_count = FOLDS // cores
-    lanes = padded(blocks * SHRINK_LEVELS, 128)
     vmem = pl.BlockSpec(memory_space=pltpu.VMEM)
     hbm = pl.BlockSpec(memory_space=pl.ANY)
     predictions, level_gram, level_cross = pl.pallas_call(
         functools.partial(kernel, (chips, cores, blocks, variants, size, traits, part)),
         out_shape=(
             jax.ShapeDtypeStruct((own_count, 1, SHRINK_LEVELS, traits, rows_fold), jnp.bfloat16),
-            jax.ShapeDtypeStruct((own_count, SHRINK_LEVELS, rows - size, lanes), jnp.float32),
-            jax.ShapeDtypeStruct((own_count, SHRINK_LEVELS, rows - size, lanes), jnp.float32),
+            jax.ShapeDtypeStruct(
+                (own_count, SHRINK_LEVELS, 1, blocks * SHRINK_LEVELS * (rows - size)), jnp.float32
+            ),
+            jax.ShapeDtypeStruct((own_count, SHRINK_LEVELS, 1, rows - size), jnp.float32),
         ),
         in_specs=[hbm, hbm, hbm, pl.BlockSpec(memory_space=pltpu.SMEM)],
         out_specs=(vmem,) * 3,
@@ -475,10 +491,11 @@
             collective_id=0, has_side_effects=True, vmem_limit_bytes=60 * 1024 * 1024
         ),
     )(allele_dosage_table, phenotype_values, individual_partition_label.reshape(1, width), shrink_strengths)
-    level_gram = level_gram[:, :, 0:traits, 0:blocks * SHRINK_LEVELS].reshape(
-        own_count, 1, SHRINK_LEVELS, traits, blocks, SHRINK_LEVELS
-    )
-    level_cross = level_cross[:, None, :, 0:traits, 0]
+    level_gram = level_gram.reshape(
+        own_count, 1, SHRINK_LEVELS, blocks, SHRINK_LEVELS, rows - size
+    )[..., 0:traits]
+    level_gram = jnp.transpose(level_gram, (0, 1, 2, 5, 3, 4))
+    level_cross = jnp.transpose(level_cross, (0, 2, 1, 3))[..., 0:traits]
     return (predictions, level_gram, level_cross)
 
 

time: 63.8 us -> 58.5 us (0.917); the launches traced: 63.5 us -> 57.4 us
  Pallas kernels: 59.3 us -> 52.1 us
  other arithmetic: 0 us -> 0.66 us
    pallas_call x1, Pallas kernels: 59.3 us -> 52.1 us  [per_device(): pl.pallas_call(functools.partial(kernel, (chips, cores, blocks, variants,...]
    slice x3 -> x0, local copies, waits for them, and re-layouts: 2.18 us -> none  [the longest x1 1.47 us: per_device(): level_cross = level_cross[:, None, :, 0:traits, 0]]
    unnamed x3 -> x6, local copies, waits for them, and re-layouts: 1.4 us -> 2.75 us
    pallas_call x0 -> x1, other arithmetic: none -> 0.66 us  [per_device(): pl.pallas_call(functools.partial(kernel, (chips, cores, blocks, variants,...]
where the time goes in v6:
time: 58.5 us; the launch traced here: 57.4 us
  Pallas kernels  52.1 us (89%)
  local copies, waits for them, and re-layouts  3.95 us (7%)
  other arithmetic  0.66 us (1%)
  between operations  0.64 us (1%)
    pallas_call x1, Pallas kernels, per_device(): pl.pallas_call(functools.partial(kernel, (chips, cores, blocks, variants,...  52.1 us
    unnamed x6, local copies, waits for them, and re-layouts  2.75 us

profile of v6, /device:TPU:0, one launch (start us, length us, event | category | flops | bytes accessed | tf_op | source)
XLA Modules:
  0.0 57.4 jit_solution(12697257116341179047)
XLA Ops:
  0.6 52.1 %shard_map.67 = (bf16[2,1,2,20,128]{4,3,2,1,0:T(8,128)(2,1)}, f32[2,2,1,128]{3,2,1,0:T(1,128)}, f32[2,2,1,32]{3,2,1,0:T(1,128)}) custom-call(bf16[500,512]{1,0:T(8,128)(2,1)} %geno_hbm.1, bf16[20,512]{1,0:T(8,128)(2,1)} %trait_hbm.1, s32[1,512]{1,0:T(1,128)} %bitcast.8, f32[2]{0:T(128)} %value_ref.1), custom_call_target="tpu_custom_call" | custom-call | tf_op jit(solution)/shard_map/pallas_call | solution.py:459
  52.7 1.4 %copy.8 = bf16[2,1,2,20,128]{4,2,3,1,0:T(2,128)(2,1)} copy(bf16[2,1,2,20,128]{4,3,2,1,0:T(8,128)(2,1)} %get-tuple-element.9) | data formatting | bytes 40960
  54.1 0.0 copy-start.1
  54.1 0.5 broadcast.3
  54.6 0.2 copy-done.1
  54.8 0.7 %reduce.3 = f32[2,2,128]{2,1,0:T(2,128)S(1)} reduce(f32[2,2,1,128]{3,2,1,0:T(1,128)S(1)} %copy-done.1, f32[]{:T(128)} %broadcast.3), dimensions={2}, to_apply=%get-tuple-element.7.reduce_sub_computation.3 | reduce | bytes 4100 | tf_op jit(solution)/shard_map/pallas_call | solution.py:459
  55.4 0.1 reshape.13
  55.5 0.6 %slice_bitcast_fusion = f32[2,1,2,20,2,2]{3,5,4,2,1,0:T(2,128)} fusion(f32[2,1,2,2,2,32]{5,4,3,2,1,0:T(2,128)S(1)} %bitcast.7), kind=kLoop, calls=%fused_computation | loop fusion | bytes 2560 | tf_op jit(solution)/shard_map/transpose | solution.py:497
  56.1 0.0 copy-start
  56.1 0.7 %copy-done = f32[2,2,1,32]{3,2,1,0:T(1,128)S(1)} copy-done((f32[2,2,1,32]{3,2,1,0:T(1,128)S(1)}, f32[2,2,1,32]{3,2,1,0:T(1,128)}, u32[]{:S(2)}) %copy-start) | copy-done | bytes 536
  56.8 0.6 %slice_bitcast_fusion.1 = f32[2,1,2,20]{3,2,1,0:T(2,128)} fusion(f32[2,1,2,32]{3,2,0,1:T(2,128)S(1)} %bitcast.9), kind=kLoop, calls=%fused_computation.1 | loop fusion | bytes 640
Async XLA Ops:
  54.1 0.7 %copy-start.1 = (f32[2,2,1,128]{3,2,1,0:T(1,128)S(1)}, f32[2,2,1,128]{3,2,1,0:T(1,128)}, u32[]{:S(2)}) copy-start(f32[2,2,1,128]{3,2,1,0:T(1,128)} %get-tuple-element.7) | copy-start | bytes 6148
  56.1 0.7 %copy-start = (f32[2,2,1,32]{3,2,1,0:T(1,128)S(1)}, f32[2,2,1,32]{3,2,1,0:T(1,128)}, u32[]{:S(2)}) copy-start(f32[2,2,1,32]{3,2,1,0:T(1,128)} %get-tuple-element.8) | copy-start | bytes 1540

commit v7 on v6

--- a/solution.py
+++ b/solution.py
@@ -29,6 +29,18 @@
     return lax.dot_general(
         left, right, (((a_dim,), (0,)), ((), ())), preferred_element_type=jnp.float32
     )
+
+
+def rows_times(a, parts):
+    count = a.shape[0]
+    stacked = jnp.concatenate(split(a), axis=0)
+    total = None
+    for n, part in enumerate(parts):
+        found = jnp.dot(stacked[0:(3 - n) * count, :], part, preferred_element_type=jnp.float32)
+        for i in range(3 - n):
+            one = found[i * count:(i + 1) * count, :]
+            total = one if total is None else total + one
+    return total
 
 
 def sweep(block, m):
@@ -232,7 +244,7 @@
             piece = jnp.concatenate([land[source, q, f] for f in range(cores)], axis=0)
             columns.append(jnp.where(fold == q, jnp.zeros_like(piece), piece))
         both = jnp.concatenate(columns, axis=1)
-        total[...] += dot_nt(both[0:size, :], both)
+        total[...] += dot_nt(both, both[0:size, :])
 
     add(z, range(FOLDS))
 
@@ -336,13 +348,14 @@
         value = jnp.where(level == r, value_ref[r], value)
     added = jnp.where(sub == lane, jnp.where(sub < variants, value, 1.0), 0.0)
     total[...] = total[...] * (1.0 / tally)
-    total[:, 0:size] = total[:, 0:size] + added
-    work[...] = total[:, 0:size]
+    total[0:size, :] = total[0:size, :] + added
+    work[...] = total[0:size, :]
     invert(work, strip, late)
-    right = total[:, size:]
-    first = dot_f32(work[...], right)
-    residual = right - dot_f32(total[:, 0:size], first)
-    betas = (first + dot_f32(work[...], residual)).astype(jnp.bfloat16)
+    right = total[size:, :]
+    inverse = split(work[...])
+    first = rows_times(right, inverse)
+    residual = right - rows_times(first, split(total[0:size, :]))
+    betas = (first + rows_times(residual, inverse)).astype(jnp.bfloat16)
 
     def late_done(distance, carry):
         def wait(source, onward, more, early, last):
@@ -357,9 +370,7 @@
     lax.fori_loop(1, chips, late_done, 0)
     for s in range(chips):
         chunk = jnp.concatenate([land[s, fold, f] for f in range(cores)], axis=0)
-        preds = lax.dot_general(
-            betas, chunk[0:size, :], (((0,), (0,)), ((), ())), preferred_element_type=jnp.float32
-        )
+        preds = jnp.dot(betas, chunk[0:size, :], preferred_element_type=jnp.float32)
         preds_ref[:, s * rows_fold:(s + 1) * rows_fold] = preds.astype(jnp.bfloat16)
 
     def message(n, t, b):
@@ -409,8 +420,12 @@
         for r in range(SHRINK_LEVELS):
             mine = slots[k, x, r]
             out_ref[k, 0, r] = slots[k, x, r, 0:traits, pl.ds(pl.multiple_of(z * rows_fold, rows_fold), rows_fold)]
-            gram_ref[k, r] = same_trait(mine, everything)
-            cross_ref[k, r] = same_trait(mine, trait)
+            found = same_trait(mine, everything)
+            for b in range(blocks):
+                for s in range(SHRINK_LEVELS):
+                    start = (b * SHRINK_LEVELS + s) * rows
+                    gram_ref[k, 0, r, b, s:s + 1, :] = found[:, start:start + traits]
+            cross_ref[k, 0, r:r + 1, :] = same_trait(mine, trait)[:, 0:traits]
 
     @pl.when(reports)
     def _():
@@ -455,15 +470,16 @@
     held = chips * rows_fold
     own_count = FOLDS // cores
     vmem = pl.BlockSpec(memory_space=pltpu.VMEM)
-    hbm = pl.BlockSpec(memory_space=pl.ANY)
+    hbm = pl.BlockSpec(memory_space=pltpu.HBM)
+    buffers = 2 * chips * (FOLDS * rows * rows_fold + own_count * blocks * SHRINK_LEVELS * (rows - size) * rows_fold)
     predictions, level_gram, level_cross = pl.pallas_call(
         functools.partial(kernel, (chips, cores, blocks, variants, size, traits, part)),
         out_shape=(
             jax.ShapeDtypeStruct((own_count, 1, SHRINK_LEVELS, traits, rows_fold), jnp.bfloat16),
             jax.ShapeDtypeStruct(
-                (own_count, SHRINK_LEVELS, 1, blocks * SHRINK_LEVELS * (rows - size)), jnp.float32
+                (own_count, 1, SHRINK_LEVELS, blocks, SHRINK_LEVELS, traits), jnp.float32
             ),
-            jax.ShapeDtypeStruct((own_count, SHRINK_LEVELS, 1, rows - size), jnp.float32),
+            jax.ShapeDtypeStruct((own_count, 1, SHRINK_LEVELS, traits), jnp.float32),
         ),
         in_specs=[hbm, hbm, hbm, pl.BlockSpec(memory_space=pltpu.SMEM)],
         out_specs=(vmem,) * 3,
@@ -473,7 +489,7 @@
             pltpu.VMEM((1, width), jnp.int32),
             pltpu.VMEM((rows, width), jnp.bfloat16),
             pltpu.VMEM((chips, FOLDS, cores, part, rows_fold), jnp.bfloat16),
-            pltpu.VMEM((size, rows), jnp.float32),
+            pltpu.VMEM((rows, size), jnp.float32),
             pltpu.VMEM((size, size), jnp.float32),
             pltpu.VMEM((PANEL, size), jnp.float32),
             pltpu.VMEM((rows - size, held), jnp.bfloat16),
@@ -488,14 +504,10 @@
             pltpu.SemaphoreType.DMA((own_count, blocks, SHRINK_LEVELS)),
         ],
         compiler_params=pltpu.CompilerParams(
-            collective_id=0, has_side_effects=True, vmem_limit_bytes=60 * 1024 * 1024
+            collective_id=0, has_side_effects=True, vmem_limit_bytes=buffers + 20 * 1024 * 1024
         ),
     )(allele_dosage_table, phenotype_values, individual_partition_label.reshape(1, width), shrink_strengths)
-    level_gram = level_gram.reshape(
-        own_count, 1, SHRINK_LEVELS, blocks, SHRINK_LEVELS, rows - size
-    )[..., 0:traits]
     level_gram = jnp.transpose(level_gram, (0, 1, 2, 5, 3, 4))
-    level_cross = jnp.transpose(level_cross, (0, 2, 1, 3))[..., 0:traits]
     return (predictions, level_gram, level_cross)
 
 

time: 58.5 us -> 55 us (0.940)
  Pallas kernels: 52.1 us -> 48.4 us
  local copies, waits for them, and re-layouts: 3.95 us -> 4.9 us
  other arithmetic: 0.66 us -> 0 us
    pallas_call x1, Pallas kernels: 52.1 us -> 48.4 us  [per_device(): pl.pallas_call(functools.partial(kernel, (chips, cores, blocks, variants,...]
    unnamed x6 -> x11, local copies, waits for them, and re-layouts: 2.75 us -> 4.9 us
    pallas_call x1 -> x0, other arithmetic: 0.66 us -> none  [per_device(): pl.pallas_call(functools.partial(kernel, (chips, cores, blocks, variants,...]
    transpose x1 -> x0, local copies, waits for them, and re-layouts: 0.6 us -> none  [per_device(): level_gram = jnp.transpose(level_gram, (0, 1, 2, 5, 3, 4))]
where the time goes in v7:
time: 55 us; the launch traced here: 53.9 us
  Pallas kernels  48.4 us (88%)
  local copies, waits for them, and re-layouts  4.9 us (9%)
  between operations  0.65 us (1%)
    pallas_call x1, Pallas kernels, per_device(): pl.pallas_call(functools.partial(kernel, (chips, cores, blocks, variants,...  48.4 us
    unnamed x11, local copies, waits for them, and re-layouts  4.9 us

profile of v7, /device:TPU:0, one launch (start us, length us, event | category | flops | bytes accessed | tf_op | source)
XLA Modules:
  0.0 53.9 jit_solution(5690640260843618948)
XLA Ops:
  0.6 0.0 copy-start.3
  0.6 0.6 %copy-done.3 = f32[2]{0:T(128)S(1)} copy-done((f32[2]{0:T(128)S(1)}, f32[2]{0:T(128)}, u32[]{:S(2)}) %copy-start.3) | copy-done | bytes 32
  1.3 0.0 copy-start
  1.3 1.0 %copy-done = bf16[500,512]{1,0:T(8,128)(2,1)S(1)} copy-done((bf16[500,512]{1,0:T(8,128)(2,1)S(1)}, bf16[500,512]{1,0:T(8,128)(2,1)}, u32[]{:S(2)}) %copy-start) | copy-done | bytes 512024
  2.3 0.0 copy-start.1
  2.3 0.7 %copy-done.1 = bf16[20,512]{1,0:T(8,128)(2,1)S(1)} copy-done((bf16[20,512]{1,0:T(8,128)(2,1)S(1)}, bf16[20,512]{1,0:T(8,128)(2,1)}, u32[]{:S(2)}) %copy-start.1) | copy-done | bytes 20504
  3.1 0.0 copy-start.2
  3.1 0.7 %copy-done.2 = s32[512]{0:T(512)S(1)} copy-done((s32[512]{0:T(512)S(1)}, s32[512]{0:T(512)}, u32[]{:S(2)}) %copy-start.2) | copy-done | bytes 2072
  3.7 48.4 %shard_map.67 = (bf16[2,1,2,20,128]{4,3,2,1,0:T(8,128)(2,1)S(1)}, f32[2,1,2,2,2,20]{5,4,3,2,1,0:T(2,128)S(1)}, f32[2,1,2,20]{3,2,1,0:T(2,128)S(1)}) custom-call(bf16[500,512]{1,0:T(8,128)(2,1)S(1)} %copy-done, bf16[20,512]{1,0:T(8,128)(2,1)S(1)} %copy-done.1, s32[1,512]{1,0:T(1,128)S(1)} %bitcast.3, f32[2]{0:T(128)S(1)} %copy-done.3), custom_call_target="tpu_custom_call" | custom-call | tf_op jit(solution)/shard_map/pallas_call | solution.py:475
  52.1 0.6 %copy.7 = bf16[2,1,2,20,128]{4,2,3,1,0:T(2,128)(2,1)} copy(bf16[2,1,2,20,128]{4,3,2,1,0:T(8,128)(2,1)S(1)} %get-tuple-element.9) | data formatting | bytes 40960
  52.7 0.6 %copy.10 = f32[2,1,2,20,2,2]{3,5,4,2,1,0:T(2,128)} copy(f32[2,1,2,20,2,2]{3,5,4,2,1,0:T(2,128)S(1)} %bitcast.2) | data formatting | bytes 2560
  53.3 0.6 %copy.11 = f32[2,1,2,20]{3,2,1,0:T(2,128)} copy(f32[2,1,2,20]{3,2,1,0:T(2,128)S(1)} %get-tuple-element.17) | data formatting | bytes 640
Async XLA Ops:
  0.6 0.7 %copy-start.3 = (f32[2]{0:T(128)S(1)}, f32[2]{0:T(128)}, u32[]{:S(2)}) copy-start(f32[2]{0:T(128)} %value_ref.1) | copy-start | bytes 28
  1.3 1.0 %copy-start = (bf16[500,512]{1,0:T(8,128)(2,1)S(1)}, bf16[500,512]{1,0:T(8,128)(2,1)}, u32[]{:S(2)}) copy-start(bf16[500,512]{1,0:T(8,128)(2,1)} %geno_hbm.1) | copy-start | bytes 1536004
  2.3 0.7 %copy-start.1 = (bf16[20,512]{1,0:T(8,128)(2,1)S(1)}, bf16[20,512]{1,0:T(8,128)(2,1)}, u32[]{:S(2)}) copy-start(bf16[20,512]{1,0:T(8,128)(2,1)} %trait_hbm.1) | copy-start | bytes 61444
  3.1 0.7 %copy-start.2 = (s32[512]{0:T(512)S(1)}, s32[512]{0:T(512)}, u32[]{:S(2)}) copy-start(s32[512]{0:T(512)} %param.6) | copy-start | bytes 6148

commit v8 on v7

--- a/solution.py
+++ b/solution.py
@@ -10,7 +10,7 @@
 SHRINK_LEVELS = 2
 FOLDS = 4
 PANEL = 128
-MINI = 16
+MINI = 32
 
 
 def split(a):
@@ -470,8 +470,7 @@
     held = chips * rows_fold
     own_count = FOLDS // cores
     vmem = pl.BlockSpec(memory_space=pltpu.VMEM)
-    hbm = pl.BlockSpec(memory_space=pltpu.HBM)
-    buffers = 2 * chips * (FOLDS * rows * rows_fold + own_count * blocks * SHRINK_LEVELS * (rows - size) * rows_fold)
+    hbm = pl.BlockSpec(memory_space=pl.ANY)
     predictions, level_gram, level_cross = pl.pallas_call(
         functools.partial(kernel, (chips, cores, blocks, variants, size, traits, part)),
         out_shape=(
@@ -504,7 +503,7 @@
             pltpu.SemaphoreType.DMA((own_count, blocks, SHRINK_LEVELS)),
         ],
         compiler_params=pltpu.CompilerParams(
-            collective_id=0, has_side_effects=True, vmem_limit_bytes=buffers + 20 * 1024 * 1024
+            collective_id=0, has_side_effects=True, vmem_limit_bytes=60 * 1024 * 1024
         ),
     )(allele_dosage_table, phenotype_values, individual_partition_label.reshape(1, width), shrink_strengths)
     level_gram = jnp.transpose(level_gram, (0, 1, 2, 5, 3, 4))

time: 55 us -> 57.2 us (1.040)
  Pallas kernels: 48.4 us -> 52.8 us
  local copies, waits for them, and re-layouts: 4.9 us -> 2.63 us
    pallas_call x1, Pallas kernels: 48.4 us -> 52.8 us  [per_device(): pl.pallas_call(functools.partial(kernel, (chips, cores, blocks, variants,...]
    unnamed x11 -> x7, local copies, waits for them, and re-layouts: 4.9 us -> 2.63 us
where the time goes in v8:
time: 57.2 us; the launch traced here: 56.1 us
  Pallas kernels  52.8 us (92%)
  local copies, waits for them, and re-layouts  2.63 us (5%)
  between operations  0.65 us (1%)
    pallas_call x1, Pallas kernels, per_device(): pl.pallas_call(functools.partial(kernel, (chips, cores, blocks, variants,...  52.8 us
    unnamed x7, local copies, waits for them, and re-layouts  2.63 us

profile of v8, /device:TPU:0, one launch (start us, length us, event | category | flops | bytes accessed | tf_op | source)
XLA Modules:
  0.0 56.1 jit_solution(8063331465491108609)
XLA Ops:
  0.6 52.8 %shard_map.67 = (bf16[2,1,2,20,128]{4,3,2,1,0:T(8,128)(2,1)}, f32[2,1,2,2,2,20]{5,4,3,2,1,0:T(2,128)}, f32[2,1,2,20]{3,2,1,0:T(2,128)}) custom-call(bf16[500,512]{1,0:T(8,128)(2,1)} %geno_hbm.1, bf16[20,512]{1,0:T(8,128)(2,1)} %trait_hbm.1, s32[1,512]{1,0:T(1,128)} %bitcast.3, f32[2]{0:T(128)} %value_ref.1), custom_call_target="tpu_custom_call" | custom-call | tf_op jit(solution)/shard_map/pallas_call | solution.py:474
  53.5 0.0 copy-start
  53.5 1.4 %copy.7 = bf16[2,1,2,20,128]{4,2,3,1,0:T(2,128)(2,1)} copy(bf16[2,1,2,20,128]{4,3,2,1,0:T(8,128)(2,1)} %get-tuple-element.9) | data formatting | bytes 40960
  54.9 0.0 copy-done
  54.9 0.0 copy-start.1
  54.9 0.6 %copy.10 = f32[2,1,2,20,2,2]{3,5,4,2,1,0:T(2,128)} copy(f32[2,1,2,20,2,2]{3,5,4,2,1,0:T(2,128)S(1)} %bitcast.2) | data formatting | bytes 2560
  55.5 0.1 copy-done.1
  55.5 0.6 %copy.11 = f32[2,1,2,20]{3,2,1,0:T(2,128)} copy(f32[2,1,2,20]{3,2,1,0:T(2,128)S(1)} %copy-done.1) | data formatting | bytes 640
Async XLA Ops:
  53.5 1.4 %copy-start = (f32[2,1,2,2,2,20]{5,4,3,2,1,0:T(2,128)S(1)}, f32[2,1,2,2,2,20]{5,4,3,2,1,0:T(2,128)}, u32[]{:S(2)}) copy-start(f32[2,1,2,2,2,20]{5,4,3,2,1,0:T(2,128)} %get-tuple-element.7) | copy-start | bytes 3844
  54.9 0.7 %copy-start.1 = (f32[2,1,2,20]{3,2,1,0:T(2,128)S(1)}, f32[2,1,2,20]{3,2,1,0:T(2,128)}, u32[]{:S(2)}) copy-start(f32[2,1,2,20]{3,2,1,0:T(2,128)} %get-tuple-element.17) | copy-start | bytes 964

commit v9 on v8

--- a/solution.py
+++ b/solution.py
@@ -10,7 +10,7 @@
 SHRINK_LEVELS = 2
 FOLDS = 4
 PANEL = 128
-MINI = 32
+MINI = 16
 
 
 def split(a):
@@ -79,29 +79,43 @@
     return jnp.concatenate(parts, axis=0)
 
 
+def invert_block(block):
+    for m in range(PANEL // MINI):
+        block = sweep(block, m)
+    return block
+
+
 def invert(work, strip, during):
     size = work.shape[0]
-
-    def panel(p, carry):
-        @pl.when(p == size // PANEL - 1)
-        def _():
-            during()
-
+    panels = size // PANEL
+
+    def panel(p, block, ahead):
         off = pl.multiple_of(p * PANEL, PANEL)
         here = pl.ds(off, PANEL)
-        block = work[here, here]
-        for m in range(PANEL // MINI):
-            block = sweep(block, m)
         sub = lax.broadcasted_iota(jnp.int32, (size, PANEL), 0)
         col = jnp.where((sub >= off) & (sub < off + PANEL), 0.0, work[:, here])
+        if ahead:
+            then = pl.ds(pl.multiple_of(off + PANEL, PANEL), PANEL)
+            above = work[here, then]
+            following = work[then, then] - dot_f32(work[then, here], dot_f32(block, above))
         work[:, here] = jnp.zeros((size, PANEL), jnp.float32)
         strip[...] = dot_f32(block, work[here, :])
         strip[:, here] = block
         work[...] = work[...] - dot_f32(col, strip[...])
         work[here, :] = strip[...]
-        return carry
-
-    lax.fori_loop(0, size // PANEL, panel, 0)
+        return invert_block(following) if ahead else block
+
+    def step(p, block):
+        @pl.when(p == panels - 2)
+        def _():
+            during()
+
+        return panel(p, block, True)
+
+    block = lax.fori_loop(0, panels - 1, step, invert_block(work[0:PANEL, 0:PANEL]))
+    if panels == 1:
+        during()
+    panel(panels - 1, block, False)
 
 
 def padded(count, multiple):
@@ -184,10 +198,7 @@
 
     stack[...] = jnp.zeros_like(stack)
     total[...] = jnp.zeros_like(total)
-    for load in loads:
-        load.wait()
-    stack[0:variants, :] = geno_ref[...]
-    stack[size:size + traits, :] = trait_ref[...]
+    loads[0].wait()
     label = label_ref[...]
     fold_row = lax.broadcasted_iota(jnp.int32, (16, width), 0)
     is_fold = fold_row == label
@@ -201,6 +212,10 @@
     target = rank + (label * rows_fold).astype(jnp.float32)
     places = lax.broadcasted_iota(jnp.int32, (width, width), 0).astype(jnp.float32)
     permute = (places == target).astype(jnp.bfloat16)
+    for load in loads[1:]:
+        load.wait()
+    stack[0:variants, :] = geno_ref[...]
+    stack[size:size + traits, :] = trait_ref[...]
     ordered = dot_nt(stack[...], permute).astype(jnp.bfloat16)
     for q in range(FOLDS):
         for f in range(cores):

time: 57.2 us -> 52.8 us (0.923)
  Pallas kernels: 52.8 us -> 48.5 us
    pallas_call x1, Pallas kernels: 52.8 us -> 48.5 us  [per_device(): pl.pallas_call(functools.partial(kernel, (chips, cores, blocks, variants,...]
where the time goes in v9:
time: 52.8 us; the launch traced here: 51.8 us
  Pallas kernels  48.5 us (92%)
  local copies, waits for them, and re-layouts  2.63 us (5%)
  between operations  0.65 us (1%)
    pallas_call x1, Pallas kernels, per_device(): pl.pallas_call(functools.partial(kernel, (chips, cores, blocks, variants,...  48.5 us
    unnamed x7, local copies, waits for them, and re-layouts  2.63 us

profile of v9, /device:TPU:0, one launch (start us, length us, event | category | flops | bytes accessed | tf_op | source)
XLA Modules:
  0.0 51.8 jit_solution(2362443347650551065)
XLA Ops:
  0.6 48.5 %shard_map.67 = (bf16[2,1,2,20,128]{4,3,2,1,0:T(8,128)(2,1)}, f32[2,1,2,2,2,20]{5,4,3,2,1,0:T(2,128)}, f32[2,1,2,20]{3,2,1,0:T(2,128)}) custom-call(bf16[500,512]{1,0:T(8,128)(2,1)} %geno_hbm.1, bf16[20,512]{1,0:T(8,128)(2,1)} %trait_hbm.1, s32[1,512]{1,0:T(1,128)} %bitcast.3, f32[2]{0:T(128)} %value_ref.1), custom_call_target="tpu_custom_call" | custom-call | tf_op jit(solution)/shard_map/pallas_call | solution.py:489
  49.2 0.0 copy-start
  49.2 1.4 %copy.7 = bf16[2,1,2,20,128]{4,2,3,1,0:T(2,128)(2,1)} copy(bf16[2,1,2,20,128]{4,3,2,1,0:T(8,128)(2,1)} %get-tuple-element.9) | data formatting | bytes 40960
  50.5 0.0 copy-done
  50.6 0.0 copy-start.1
  50.6 0.6 %copy.10 = f32[2,1,2,20,2,2]{3,5,4,2,1,0:T(2,128)} copy(f32[2,1,2,20,2,2]{3,5,4,2,1,0:T(2,128)S(1)} %bitcast.2) | data formatting | bytes 2560
  51.2 0.1 copy-done.1
  51.2 0.6 %copy.11 = f32[2,1,2,20]{3,2,1,0:T(2,128)} copy(f32[2,1,2,20]{3,2,1,0:T(2,128)S(1)} %copy-done.1) | data formatting | bytes 640
Async XLA Ops:
  49.2 1.4 %copy-start = (f32[2,1,2,2,2,20]{5,4,3,2,1,0:T(2,128)S(1)}, f32[2,1,2,2,2,20]{5,4,3,2,1,0:T(2,128)}, u32[]{:S(2)}) copy-start(f32[2,1,2,2,2,20]{5,4,3,2,1,0:T(2,128)} %get-tuple-element.7) | copy-start | bytes 3844
  50.6 0.7 %copy-start.1 = (f32[2,1,2,20]{3,2,1,0:T(2,128)S(1)}, f32[2,1,2,20]{3,2,1,0:T(2,128)}, u32[]{:S(2)}) copy-start(f32[2,1,2,20]{3,2,1,0:T(2,128)} %get-tuple-element.17) | copy-start | bytes 964

commit v10 on v9

--- a/solution.py
+++ b/solution.py
@@ -54,7 +54,10 @@
     run = jnp.where(inside, jnp.where(lane - low == sub, 1.0, 0.0), rows)
     scale = jnp.zeros((MINI, size), jnp.float32)
     for j in range(MINI):
-        inv = 1.0 / cols[j][j:j + 1, :]
+        pivot = cols[j][j:j + 1, :]
+        inv = pl.reciprocal(pivot, approx=True)
+        for _ in range(2):
+            inv = inv * (2.0 - pivot * inv)
         here = sub == j
         scale = jnp.where(here, inv, scale)
         ratio = jnp.where(here, 0.0, cols[j]) * inv

time: 52.8 us -> 55.6 us (1.053)
  Pallas kernels: 48.5 us -> 51.3 us
    pallas_call x1, Pallas kernels: 48.5 us -> 51.3 us  [per_device(): pl.pallas_call(functools.partial(kernel, (chips, cores, blocks, variants,...]
where the time goes in v10:
time: 55.6 us; the launch traced here: 54.6 us
  Pallas kernels  51.3 us (92%)
  local copies, waits for them, and re-layouts  2.63 us (5%)
  between operations  0.65 us (1%)
    pallas_call x1, Pallas kernels, per_device(): pl.pallas_call(functools.partial(kernel, (chips, cores, blocks, variants,...  51.3 us
    unnamed x7, local copies, waits for them, and re-layouts  2.63 us

profile of v10, /device:TPU:0, one launch (start us, length us, event | category | flops | bytes accessed | tf_op | source)
XLA Modules:
  0.0 54.6 jit_solution(10350298938196140827)
XLA Ops:
  0.6 51.3 %shard_map.67 = (bf16[2,1,2,20,128]{4,3,2,1,0:T(8,128)(2,1)}, f32[2,1,2,2,2,20]{5,4,3,2,1,0:T(2,128)}, f32[2,1,2,20]{3,2,1,0:T(2,128)}) custom-call(bf16[500,512]{1,0:T(8,128)(2,1)} %geno_hbm.1, bf16[20,512]{1,0:T(8,128)(2,1)} %trait_hbm.1, s32[1,512]{1,0:T(1,128)} %bitcast.3, f32[2]{0:T(128)} %value_ref.1), custom_call_target="tpu_custom_call" | custom-call | tf_op jit(solution)/shard_map/pallas_call | solution.py:492
  52.0 0.0 copy-start
  52.0 1.4 %copy.7 = bf16[2,1,2,20,128]{4,2,3,1,0:T(2,128)(2,1)} copy(bf16[2,1,2,20,128]{4,3,2,1,0:T(8,128)(2,1)} %get-tuple-element.9) | data formatting | bytes 40960
  53.3 0.0 copy-done
  53.3 0.0 copy-start.1
  53.3 0.6 %copy.10 = f32[2,1,2,20,2,2]{3,5,4,2,1,0:T(2,128)} copy(f32[2,1,2,20,2,2]{3,5,4,2,1,0:T(2,128)S(1)} %bitcast.2) | data formatting | bytes 2560
  53.9 0.1 copy-done.1
  54.0 0.6 %copy.11 = f32[2,1,2,20]{3,2,1,0:T(2,128)} copy(f32[2,1,2,20]{3,2,1,0:T(2,128)S(1)} %copy-done.1) | data formatting | bytes 640
Async XLA Ops:
  52.0 1.4 %copy-start = (f32[2,1,2,2,2,20]{5,4,3,2,1,0:T(2,128)S(1)}, f32[2,1,2,2,2,20]{5,4,3,2,1,0:T(2,128)}, u32[]{:S(2)}) copy-start(f32[2,1,2,2,2,20]{5,4,3,2,1,0:T(2,128)} %get-tuple-element.7) | copy-start | bytes 3844
  53.3 0.7 %copy-start.1 = (f32[2,1,2,20]{3,2,1,0:T(2,128)S(1)}, f32[2,1,2,20]{3,2,1,0:T(2,128)}, u32[]{:S(2)}) copy-start(f32[2,1,2,20]{3,2,1,0:T(2,128)} %get-tuple-element.17) | copy-start | bytes 964
